TPU v7x, 512 devices: a whole 4x4x16 slice. The times are simulated.
512 devices in a mesh: section: 4 (over x), tensor: 8 (over y, core), dp: 16 (over z).
Axes of the slice: x: 4, y: 4, z: 16, core: 2. Of those that a mesh axis runs over, the one named last changes fastest.
Arguments:
- inputs: bfloat16 [4, 640, 3072], P(None, 'dp', 'tensor'), may hold values from -6 to 6
- velocity_ref: bfloat16 [4, 640, 3072], P(None, 'dp', 'tensor'), may hold values from -6 to 6
- proj_weights: bfloat16 [4, 3072, 3072], P('section', 'dp', 'tensor'), may hold values from -0.109375 to 0.109375
- section_norm_gains: float32 [4, 3072], P('section'), may hold values from 0.5 to 1.5
- gate_values: float32 [4, 3072], P('section', 'tensor'), may hold values from -4 to 4
- clip_lengths: int32 [16, 4], P('dp'), may hold values from 1 to 40, 100 in all within a row
- step_indices: int32 [16, 4], P('dp'), may hold values from 0 to 49
Outputs:
- grad_weight: float32 [4, 3072, 3072], P('section', 'dp', 'tensor')
- grad_gain: float32 [4, 3072], P('section', 'tensor')
- grad_gate: float32 [4, 3072], P('section', 'tensor')
Inputs may be any that keep to these rules, and one draw needn't show every extreme that they name: `clip_lengths`: each clip's lengths over the 4 micro-batches add up to 100, and its longest is exactly 40.
All inputs are finite; a program needn't handle non-finite values.
Results may differ from a plain program's by a relative error of at most 0.02.
Values may be sent and summed in bfloat16 or wider, within the bound.
A program may use at most 128 MiB of HBM per device.

v0:
```python
import math

import jax
import jax.numpy as jnp
from jax import lax
from jax.sharding import PartitionSpec as P

NSTEPS = 50
CLIP_LIVE = 100


EPS = 1e-06


def passed_along(block, axis, distance):
    devices = range(lax.axis_size(axis))
    route = [(i - distance, i) for i in devices if i - distance in devices]
    return lax.ppermute(block, axis, route)


def gelu_slope(values):
    coeff = math.sqrt(2.0 / math.pi)
    tanh_val = jnp.tanh(coeff * (values + 0.044715 * values * values * values))
    return 0.5 * (1.0 + tanh_val) + 0.5 * values * (1.0 - tanh_val * tanh_val) * coeff * (
        1.0 + 3.0 * 0.044715 * values * values
    )


def write_position(buffer, where_at, value, live_flag):
    older = lax.dynamic_index_in_dim(buffer, where_at, 0, keepdims=False)
    newer = jnp.where(live_flag, value, older)
    return lax.dynamic_update_index_in_dim(buffer, newer, where_at, 0)


def local(
    inputs, velocity_ref, proj_weights, section_norm_gains, gate_values, clip_lengths, step_indices
):
    section_count = lax.axis_size("section")
    my_section = lax.axis_index("section")
    owned_column = lax.axis_index("tensor")
    microbatch_count = inputs.shape[0]
    count_of_rows = inputs.shape[1]
    shard_width = inputs.shape[2]
    gain_vector = section_norm_gains[0]
    gate_vec = gate_values[0]
    hidden_width = gain_vector.shape[0]
    live_total = CLIP_LIVE * lax.axis_size("dp")
    owned_gain = lax.dynamic_slice_in_dim(gain_vector, owned_column * shard_width, shard_width)
    positions = jnp.arange(count_of_rows, dtype=jnp.int32)
    live_mask = (positions[None, :] < clip_lengths[0][:, None]).astype(jnp.float32)
    weighting = 1.0 / (0.1 + (step_indices[0].astype(jnp.float32) + 0.5) / NSTEPS)
    factor = live_mask * weighting[:, None] / math.sqrt(live_total)
    full_weight = lax.all_gather(proj_weights[0], "dp", axis=0, tiled=True)
    tick_count = microbatch_count + section_count - 1
    standardized_buffer = jnp.zeros((microbatch_count, count_of_rows, hidden_width), jnp.float32)
    scale_buf = jnp.zeros((microbatch_count, count_of_rows, 1), jnp.float32)
    proj_buf = jnp.zeros((microbatch_count, count_of_rows, shard_width), jnp.float32)
    grad_buf = jnp.zeros((microbatch_count, count_of_rows, shard_width), jnp.bfloat16)
    outgoing = jnp.zeros((count_of_rows, shard_width), jnp.bfloat16)
    for tick_no in range(tick_count):
        micro_at = tick_no - my_section
        live_flag = (micro_at >= 0) & (micro_at < microbatch_count)
        read_position = jnp.clip(micro_at, 0, microbatch_count - 1)
        start_rows = lax.dynamic_index_in_dim(inputs, read_position, 0, keepdims=False)
        if tick_no > 0:
            arrived = passed_along(outgoing, "section", 1)
        else:
            arrived = outgoing
        arriving_input = jnp.where(my_section == 0, start_rows, arrived)
        gathered = lax.all_gather(arriving_input, "tensor", axis=1, tiled=True).astype(jnp.float32)
        mean_val = jnp.mean(gathered, axis=-1, keepdims=True)
        mean_removed = gathered - mean_val
        inverse_deviation = lax.rsqrt(
            jnp.mean(mean_removed * mean_removed, axis=-1, keepdims=True) + EPS
        )
        standardized = mean_removed * inverse_deviation
        normed_rows = (standardized * gain_vector).astype(jnp.bfloat16)
        projection_output = jnp.dot(normed_rows, full_weight, preferred_element_type=jnp.float32)
        result_rows = (
            arriving_input.astype(jnp.float32)
            + gate_vec * jax.nn.gelu(projection_output, approximate=True)
        ).astype(jnp.bfloat16)
        target = lax.dynamic_index_in_dim(velocity_ref, read_position, 0, keepdims=False).astype(
            jnp.float32
        )
        row_factor = lax.dynamic_index_in_dim(factor, read_position, 0, keepdims=False)
        start_grad = (row_factor[:, None] * (result_rows.astype(jnp.float32) - target)).astype(
            jnp.bfloat16
        )
        standardized_buffer = write_position(
            standardized_buffer, read_position, standardized, live_flag
        )
        scale_buf = write_position(scale_buf, read_position, inverse_deviation, live_flag)
        proj_buf = write_position(proj_buf, read_position, projection_output, live_flag)
        grad_buf = write_position(grad_buf, read_position, start_grad, live_flag)
        outgoing = result_rows
    back_weight = lax.all_gather(proj_weights[0], "dp", axis=0, tiled=True)
    weight_acc = jnp.zeros((hidden_width, shard_width), jnp.float32)
    gate_acc = jnp.zeros((shard_width,), jnp.float32)
    gain_accumulator = jnp.zeros((shard_width,), jnp.float32)
    returning = jnp.zeros((count_of_rows, shard_width), jnp.bfloat16)
    for tick_no in range(tick_count):
        micro_at = tick_no - (section_count - 1 - my_section)
        live_flag = (micro_at >= 0) & (micro_at < microbatch_count)
        read_position = jnp.clip(micro_at, 0, microbatch_count - 1)
        if tick_no > 0:
            arrived = passed_along(returning, "section", -1)
        else:
            arrived = returning
        own_start = lax.dynamic_index_in_dim(grad_buf, read_position, 0, keepdims=False)
        upstream_gradient = jnp.where(my_section == section_count - 1, own_start, arrived).astype(
            jnp.float32
        )
        standardized = lax.dynamic_index_in_dim(
            standardized_buffer, read_position, 0, keepdims=False
        )
        inverse_deviation = lax.dynamic_index_in_dim(scale_buf, read_position, 0, keepdims=False)
        projection_output = lax.dynamic_index_in_dim(proj_buf, read_position, 0, keepdims=False)
        gate_acc = gate_acc + jnp.where(
            live_flag,
            jnp.sum(upstream_gradient * jax.nn.gelu(projection_output, approximate=True), axis=0),
            0.0,
        )
        dproj = (upstream_gradient * gate_vec * gelu_slope(projection_output)).astype(jnp.bfloat16)
        normed_rows = (standardized * gain_vector).astype(jnp.bfloat16)
        weight_term = lax.dot_general(
            normed_rows, dproj, (((0,), (0,)), ((), ())), preferred_element_type=jnp.float32
        )
        weight_acc = weight_acc + jnp.where(live_flag, weight_term, 0.0)
        partial_value = lax.dot_general(
            dproj, back_weight, (((1,), (1,)), ((), ())), preferred_element_type=jnp.float32
        )
        owned_standardized = lax.dynamic_slice_in_dim(
            standardized, owned_column * shard_width, shard_width, 1
        )
        summed = lax.psum(partial_value.astype(jnp.bfloat16), "tensor").astype(jnp.float32)
        scaled_rows = summed * gain_vector
        first_moment = jnp.mean(scaled_rows, axis=-1, keepdims=True)
        second_moment = jnp.mean(scaled_rows * standardized, axis=-1, keepdims=True)
        owned_gradient = lax.dynamic_slice_in_dim(
            summed, owned_column * shard_width, shard_width, 1
        )
        gain_accumulator = gain_accumulator + jnp.where(
            live_flag, jnp.sum(owned_gradient * owned_standardized, axis=0), 0.0
        )
        input_gradient = upstream_gradient + inverse_deviation * (
            owned_gradient * owned_gain - first_moment - owned_standardized * second_moment
        )
        returning = input_gradient.astype(jnp.bfloat16)
    weight_sum = lax.psum_scatter(
        weight_acc.astype(jnp.bfloat16), "dp", scatter_dimension=0, tiled=True
    ).astype(jnp.float32)
    gate_sum, gain_sum = lax.psum((gate_acc, gain_accumulator), "dp")
    return (weight_sum[None], gain_sum[None], gate_sum[None])


def solution(mesh):
    placed = (
        P(None, "dp", "tensor"),
        P(None, "dp", "tensor"),
        P("section", "dp", "tensor"),
        P("section", None),
        P("section", "tensor"),
        P("dp", None),
        P("dp", None),
    )
    return jax.shard_map(
        local,
        mesh=mesh,
        in_specs=placed,
        out_specs=(P("section", "dp", "tensor"), P("section", "tensor"), P("section", "tensor")),
        check_vma=False,
    )
```

profile of v0, /device:TPU:16, one launch (start us, length us, event | category | flops | bytes accessed | tf_op | source)
XLA Modules:
  0.0 885.3 jit_solution(9070595736559612980)
XLA Ops:
  10.2 16.5 %all-gather = bf16[1,40,3072]{2,1,0:T(8,128)(2,1)S(1)} all-gather(bf16[1,40,384]{2,1,0:T(8,128)(2,1)S(1)} %dynamic-slice_select_fusion.1), channel_id=2, replica_groups=mesh['section'=4,'tensor'=8,'dp'=16] {'tensor'}, dimensions={2}, use_global_device_ids=true | all-gather | bytes 276480 | tf_op jit(solution)/shard_map/all_gather | solution.py:70
  30.7 57.8 %all-gather.4.cloned.1.call-done = bf16[1,3072,384]{2,1,0:T(8,128)(2,1)} async-done(((bf16[1,192,384]{2,1,0:T(8,128)(2,1)}), bf16[1,3072,384]{2,1,0:T(8,128)(2,1)}) %all-gather.4.cloned.1.call-update) | async-done | bytes 2359312 | tf_op jit(solution)/shard_map/all_gather | solution.py:53
  95.9 11.6 %all_gather.27 = bf16[40,3072]{1,0:T(8,128)(2,1)S(1)} all-gather(bf16[40,384]{1,0:T(8,128)(2,1)S(1)} %bitcast_select_fusion.17), channel_id=1, replica_groups=mesh['section'=4,'tensor'=8,'dp'=16] {'tensor'}, dimensions={1}, use_global_device_ids=true | all-gather | bytes 276480 | tf_op jit(solution)/shard_map/all_gather | solution.py:70
  114.4 12.9 %all_gather.28 = bf16[40,3072]{1,0:T(8,128)(2,1)S(1)} all-gather(bf16[40,384]{1,0:T(8,128)(2,1)S(1)} %bitcast_select_fusion.16), channel_id=1, replica_groups=mesh['section'=4,'tensor'=8,'dp'=16] {'tensor'}, dimensions={1}, use_global_device_ids=true | all-gather | bytes 276480 | tf_op jit(solution)/shard_map/all_gather | solution.py:70
  128.2 4.2 collective-permute-start.2
  134.0 12.9 %all_gather.29 = bf16[40,3072]{1,0:T(8,128)(2,1)S(1)} all-gather(bf16[40,384]{1,0:T(8,128)(2,1)S(1)} %bitcast_select_fusion.15), channel_id=1, replica_groups=mesh['section'=4,'tensor'=8,'dp'=16] {'tensor'}, dimensions={1}, use_global_device_ids=true | all-gather | bytes 276480 | tf_op jit(solution)/shard_map/all_gather | solution.py:70
  147.8 4.2 collective-permute-start.3
  153.7 12.9 %all_gather.30 = bf16[40,3072]{1,0:T(8,128)(2,1)S(1)} all-gather(bf16[40,384]{1,0:T(8,128)(2,1)S(1)} %bitcast_select_fusion.14), channel_id=1, replica_groups=mesh['section'=4,'tensor'=8,'dp'=16] {'tensor'}, dimensions={1}, use_global_device_ids=true | all-gather | bytes 276480 | tf_op jit(solution)/shard_map/all_gather | solution.py:70
  167.5 4.2 collective-permute-start.4
  173.3 12.9 %all_gather.31 = bf16[40,3072]{1,0:T(8,128)(2,1)S(1)} all-gather(bf16[40,384]{1,0:T(8,128)(2,1)S(1)} %bitcast_select_fusion.13), channel_id=1, replica_groups=mesh['section'=4,'tensor'=8,'dp'=16] {'tensor'}, dimensions={1}, use_global_device_ids=true | all-gather | bytes 276480 | tf_op jit(solution)/shard_map/all_gather | solution.py:70
  193.0 12.9 %all_gather.32 = bf16[40,3072]{1,0:T(8,128)(2,1)S(1)} all-gather(bf16[40,384]{1,0:T(8,128)(2,1)S(1)} %bitcast_select_fusion.12), channel_id=1, replica_groups=mesh['section'=4,'tensor'=8,'dp'=16] {'tensor'}, dimensions={1}, use_global_device_ids=true | all-gather | bytes 276480 | tf_op jit(solution)/shard_map/all_gather | solution.py:70
  210.5 68.4 %all-reduce.9.cloned.1.call-done = bf16[40,3072]{1,0:T(8,128)(2,1)} async-done(((bf16[40,3072]{1,0:T(8,128)(2,1)}), bf16[40,3072]{1,0:T(8,128)(2,1)}) %all-reduce.9.cloned.1.call-update) | async-done | bytes 245776 | tf_op jit(solution)/shard_map/psum | solution.py:136
  283.6 4.5 collective-permute-done.6
  289.9 74.3 %all-reduce.11.cloned.1.call-done = bf16[40,3072]{1,0:T(8,128)(2,1)} async-done(((bf16[40,3072]{1,0:T(8,128)(2,1)}), bf16[40,3072]{1,0:T(8,128)(2,1)}) %all-reduce.11.cloned.1.call-update) | async-done | bytes 245776 | tf_op jit(solution)/shard_map/psum | solution.py:136
  369.6 4.5 collective-permute-done.7
  375.9 74.3 %all-reduce.13.cloned.1.call-done = bf16[40,3072]{1,0:T(8,128)(2,1)} async-done(((bf16[40,3072]{1,0:T(8,128)(2,1)}), bf16[40,3072]{1,0:T(8,128)(2,1)}) %all-reduce.13.cloned.1.call-update) | async-done | bytes 245776 | tf_op jit(solution)/shard_map/psum | solution.py:136
  455.7 4.4 collective-permute-done.8
  465.9 70.3 %all-reduce.15.cloned.1.call-done = bf16[40,3072]{1,0:T(8,128)(2,1)} async-done(((bf16[40,3072]{1,0:T(8,128)(2,1)}), bf16[40,3072]{1,0:T(8,128)(2,1)}) %all-reduce.15.cloned.1.call-update) | async-done | bytes 245776 | tf_op jit(solution)/shard_map/psum | solution.py:136
  552.1 70.9 %all-reduce.17.cloned.1.call-done = bf16[40,3072]{1,0:T(8,128)(2,1)} async-done(((bf16[40,3072]{1,0:T(8,128)(2,1)}), bf16[40,3072]{1,0:T(8,128)(2,1)}) %all-reduce.17.cloned.1.call-update) | async-done | bytes 245776 | tf_op jit(solution)/shard_map/psum | solution.py:136
  638.8 71.0 %all-reduce.19.cloned.1.call-done = bf16[40,3072]{1,0:T(8,128)(2,1)} async-done(((bf16[40,3072]{1,0:T(8,128)(2,1)}), bf16[40,3072]{1,0:T(8,128)(2,1)}) %all-reduce.19.cloned.1.call-update) | async-done | bytes 245776 | tf_op jit(solution)/shard_map/psum | solution.py:136
  721.9 9.1 %add_convert_fusion = bf16[3072,384]{1,0:T(8,128)(2,1)} fusion(f32[3072,384]{1,0:T(8,128)} %fusion.101, f32[3072,384]{1,0:T(8,128)} %fusion.99, f32[3072,384]{1,0:T(8,128)} %fusion.97, f32[3072,384]{1,0:T(8,128)} %fusion.95, f32[3072,384]{1,0:T(8,128)} %fusion.93, f32[3072,384]{1,0:T(8,128)} %fusion.91, bf16[40,384]{1,0:T(8,128)(2,1)S(1)} %get-tuple-element.43, ...), kind=kOutput, calls=%fused_computation | convolution fusion | flops 111132672 | bytes 31205388 | tf_op jit(solution)/shard_map/dot_general | solution.py:126
  731.0 65.8 %all-reduce.21.cloned.1.call-done = bf16[40,3072]{1,0:T(8,128)(2,1)} async-done(((bf16[40,3072]{1,0:T(8,128)(2,1)}), bf16[40,3072]{1,0:T(8,128)(2,1)}) %all-reduce.21.cloned.1.call-update) | async-done | bytes 245776 | tf_op jit(solution)/shard_map/psum | solution.py:136
  798.2 31.8 %all-reduce = (f32[1,384]{1,0:T(1,128)}, f32[1,384]{1,0:T(1,128)}) all-reduce(f32[1,384]{1,0:T(1,128)S(1)} %broadcast_in_dim.195, f32[1,384]{1,0:T(1,128)S(1)} %broadcast_in_dim.196), channel_id=1, replica_groups=mesh['section'=4,'tensor'=8,'dp'=16] {'dp'}, use_global_device_ids=true, to_apply=%region_41.42 | all-reduce | flops 768 | bytes 6144 | tf_op jit(solution)/shard_map/psum | solution.py:153
  830.1 47.0 %reduce-scatter.2.cloned.1.call-done = bf16[192,384]{1,0:T(8,128)(2,1)} async-done(((bf16[3072,384]{1,0:T(8,128)(2,1)}), bf16[192,384]{1,0:T(8,128)(2,1)}) %reduce-scatter.2.cloned.1.call-update) | async-done | bytes 147472 | tf_op jit(solution)/shard_map/reduce_scatter | solution.py:150
  (207 shorter events, 111.5 us)
Async XLA Ops:
  7.2 81.2 %all-gather.4.cloned.1.call-start = ((), (), s32[]{:S(2)}) async-start(), calls=%async_computation.9 | async-start | bytes 2506752 | tf_op jit(solution)/shard_map/all_gather | solution.py:53
  7.9 271.0 %all-reduce.9.cloned.1.call-start = ((), (), s32[]{:S(2)}) async-start(), calls=%async_computation.1 | async-start | bytes 491520 | tf_op jit(solution)/shard_map/psum | solution.py:136
  8.0 80.4 %copy-start.4 = (f32[1,3072]{1,0:T(1,128)S(1)}, f32[1,3072]{1,0:T(1,128)}, u32[]{:S(2)}) copy-start(f32[1,3072]{1,0:T(1,128)} %param.10) | copy-start | bytes 36868
  8.0 80.4 %copy-start.11 = (bf16[4,40,384]{2,1,0:T(8,128)(2,1)S(1)}, bf16[4,40,384]{2,1,0:T(8,128)(2,1)}, u32[]{:S(2)}) copy-start(bf16[4,40,384]{2,1,0:T(8,128)(2,1)} %param.8) | copy-start | bytes 368644
  29.4 66.5 %copy-start.10 = (bf16[4,40,384]{2,1,0:T(8,128)(2,1)S(1)}, bf16[4,40,384]{2,1,0:T(8,128)(2,1)}, u32[]{:S(2)}) copy-start(bf16[4,40,384]{2,1,0:T(8,128)(2,1)} %param.7) | copy-start | bytes 368644
  90.8 5.1 collective-permute-start
  108.6 5.8 collective-permute-start.1
  128.2 5.8 collective-permute-start.2
  147.8 5.8 collective-permute-start.3
  167.5 5.8 collective-permute-start.4
  187.2 5.8 collective-permute-start.5
  209.4 154.8 %all-reduce.11.cloned.1.call-start = ((), (), s32[]{:S(2)}) async-start(), calls=%async_computation.2 | async-start | bytes 491520 | tf_op jit(solution)/shard_map/psum | solution.py:136
  282.3 5.8 collective-permute-start.6
  289.8 160.4 %all-reduce.13.cloned.1.call-start = ((), (), s32[]{:S(2)}) async-start(), calls=%async_computation.3 | async-start | bytes 491520 | tf_op jit(solution)/shard_map/psum | solution.py:136
  368.3 5.8 collective-permute-start.7
  375.8 160.4 %all-reduce.15.cloned.1.call-start = ((), (), s32[]{:S(2)}) async-start(), calls=%async_computation.4 | async-start | bytes 491520 | tf_op jit(solution)/shard_map/psum | solution.py:136
  454.3 5.8 collective-permute-start.8
  461.9 161.1 %all-reduce.17.cloned.1.call-start = ((), (), s32[]{:S(2)}) async-start(), calls=%async_computation.5 | async-start | bytes 491520 | tf_op jit(solution)/shard_map/psum | solution.py:136
  540.4 5.8 collective-permute-start.9
  547.9 161.8 %all-reduce.19.cloned.1.call-start = ((), (), s32[]{:S(2)}) async-start(), calls=%async_computation.6 | async-start | bytes 491520 | tf_op jit(solution)/shard_map/psum | solution.py:136
  627.1 5.8 collective-permute-start.10
  634.7 162.1 %all-reduce.21.cloned.1.call-start = ((), (), s32[]{:S(2)}) async-start(), calls=%async_computation.8 | async-start | bytes 491520 | tf_op jit(solution)/shard_map/psum | solution.py:136
  713.9 5.8 collective-permute-start.11
  721.7 155.4 %reduce-scatter.2.cloned.1.call-start = ((), (), s32[]{:S(2)}) async-start(), calls=%async_computation.7 | async-start | bytes 2506752 | tf_op jit(solution)/shard_map/reduce_scatter | solution.py:150
  (10 other events, 67.6 us)
Sparse Core Ops, SparseCore 0:
  10.1 78.2 all-gather.3
  209.5 69.3 all-reduce.8
  289.9 74.1 all-reduce.10
  376.0 74.1 all-reduce.12
  462.0 74.1 all-reduce.14
  548.0 74.9 all-reduce.16
  634.8 74.8 all-reduce.18
  721.8 74.9 all-reduce.20
  799.9 77.1 reduce-scatter.1
where the time goes:
time: 887 us; the launch traced here: 885 us
  waiting for transfers between devices  622 us (70%)
  blocking collectives  124 us (14%)
  matrix products  51.1 us (6%)
  starting transfers between devices  33.2 us (4%)
  other arithmetic  31.9 us (4%)
  between operations  14.7 us (2%)
    psum x7, waiting for transfers between devices, local(): lax.psum(partial_value.astype(jnp.bfloat16), 'tensor').astype(jnp.float32)  495 us
    all_gather x7, blocking collectives, local(): lax.all_gather(arriving_input, 'tensor', axis=1, tiled=True)  92.4 us
    all_gather x1, waiting for transfers between devices, local(): full_weight = lax.all_gather(proj_weights[0], 'dp', axis=0, tiled=True)  57.8 us
    reduce_scatter x1, waiting for transfers between devices, local(): lax.psum_scatter(weight_acc.astype(jnp.bfloat16), 'dp', scatter_dimension...  47 us
    dot_general x7, matrix products, local(): lax.dot_general(normed_rows, dproj, (((0,), (0,)), ((), ())), preferred_e...  33.3 us
    ppermute x12, starting transfers between devices, passed_along(): return lax.ppermute(block, axis, route)  32.4 us
    psum x1, blocking collectives, local(): gate_sum, gain_sum = lax.psum((gate_acc, gain_accumulator), 'dp')  31.8 us
    ppermute x12, waiting for transfers between devices, passed_along(): return lax.ppermute(block, axis, route)  21.4 us
  transfers between devices with their start and end apart: 21, of which 21 were waited for; matrix products, arithmetic and copies ran while one was open for 5% of the time, Pallas kernels for 0%

commit v1 on v0

v1 whole, which is shorter than its diff:
```python
import functools
import math

import jax
import jax.numpy as jnp
from jax import lax
from jax.experimental import pallas as pl
from jax.experimental.pallas import tpu as pltpu
from jax.sharding import PartitionSpec as P

MESH = pl.DeviceIdType.MESH
F32 = jnp.float32
BF16 = jnp.bfloat16
NSTEPS = 50
LIVE_PER_CLIP = 100
EPS = 1e-06
LANES = 128
HALVES = 2
SMALL_ROWS = 24
TAIL = 16
PARTS_AT = 124
LAG = 3


def split3(value):
    first = value.astype(BF16)
    rest = value - first.astype(F32)
    second = rest.astype(BF16)
    third = (rest - second.astype(F32)).astype(BF16)
    return first, second, third


def stat_rows(one, two):
    rows = [r.astype(F32) for r in split3(one) + split3(two)]
    rows.append(jnp.zeros((TAIL - 6, LANES), F32))
    return jnp.concatenate(rows, axis=0).astype(BF16)


def joined(block):
    block = block.astype(F32)
    one = block[0:1] + block[1:2] + block[2:3]
    two = block[3:4] + block[4:5] + block[5:6]
    return one, two


def kernel(
    nx, nt, nz,
    w_in, inputs, velocity, gains, gates, lengths, steps,
    gw_out, gain_out, gate_out,
    wbuf, wt, small_src, small, gainb, gtail, gateb, picked, abuf, bsend, bbuf,
    projb, gelub, slopeb, meanb, invb, ub, dbuf, qsend, qbuf, dwbuf, rs_up, rs_down,
    gw_send, gw_in, vacc, v1, v2, v3,
    send_sem, local_sem, w_sem, small_sem, up_sem, down_sem, a_sem, b_sem, d_sem, q_sem,
    rsu_sem, rsd_sem, gw_sem, v1_sem, v2_sem, v3_sem,
):
    sections = nx
    chunk = gates.shape[1] // (HALVES * nx)
    width = gates.shape[1]
    own = HALVES * chunk
    deep = nt * own
    model = nt * width
    ups, downs = nz // 2, nz // 2 - 1
    zb = 4
    za = nz // zb
    x = lax.axis_index("section")
    t = lax.axis_index("tensor")
    z = lax.axis_index("dp")
    above = lax.rem(z + 1, nz)
    below = lax.rem(z + nz - 1, nz)
    group, member = z // zb, lax.rem(z, zb)

    small[...] = jnp.zeros_like(small)
    barrier = pltpu.get_barrier_semaphore()
    greeted = 0

    def greet(axis, index):
        pl.semaphore_signal(barrier, inc=1, device_id={axis: index}, device_id_type=MESH)

    for d in range(1, nx):
        greet("section", lax.rem(x + d, nx))
        greeted += 1
    greet("dp", above)
    greet("dp", below)
    greeted += 2
    for d in range(1, nt):
        greet("tensor", lax.rem(t + d, nt))
        greeted += 1
    for d in range(1, zb):
        greet("dp", group * zb + lax.rem(member + d, zb))
        greeted += 1
    for d in range(1, za):
        greet("dp", lax.rem(group + d, za) * zb + member)
        greeted += 1

    sends = []

    def put(src, dst, recv, axis, index):
        copy = pltpu.make_async_remote_copy(
            src_ref=src, dst_ref=dst, send_sem=send_sem.at[len(sends)], recv_sem=recv,
            device_id={axis: index}, device_id_type=MESH,
        )
        copy.start()
        sends.append(copy)

    def got(dst, recv):
        pltpu.make_async_remote_copy(
            src_ref=dst, dst_ref=dst, send_sem=send_sem.at[0], recv_sem=recv,
            device_id={"dp": above}, device_id_type=MESH,
        ).wait_recv()

    own_rows = pl.ds(pl.multiple_of(x * chunk, 16), chunk)
    keep = pltpu.make_async_copy(w_in.at[0, own_rows], wbuf.at[x, z], local_sem.at[0])
    keep.start()
    small_src[...] = jnp.zeros_like(small_src)
    for to in range(nx):
        for unit in range(nz):
            at = unit * (width // HALVES) + to * chunk
            small_src[to, unit:unit + 1, 0:chunk] = gains[0:1, at:at + chunk]
        for half in range(HALVES):
            at = half * (width // HALVES) + to * chunk
            small_src[to, 16 + half:17 + half, 0:chunk] = gates[0:1, at:at + chunk]

    pl.semaphore_wait(barrier, greeted)

    for d in range(1, nx):
        to = lax.rem(x + d, nx)
        rows = pl.ds(pl.multiple_of(to * chunk, 16), chunk)
        put(w_in.at[0, rows], wbuf.at[x, z], w_sem.at[x], "section", to)
    small_at = pl.ds(pl.multiple_of(x * SMALL_ROWS, 8), SMALL_ROWS)
    for d in range(1, nx):
        to = lax.rem(x + d, nx)
        put(small_src.at[to], small.at[small_at], small_sem.at[x], "section", to)
    small[small_at] = small_src[x]
    keep.wait()

    def wait_piece(s):
        @pl.when(x != s)
        def _():
            got(wbuf.at[s, z], w_sem.at[s])

    def gather_send(s, k):
        if k <= ups:
            piece = wbuf.at[s, lax.rem(z - k + 1 + nz, nz)]
            put(piece, piece, up_sem.at[s, k - 1], "dp", above)
        if k <= downs:
            piece = wbuf.at[s, lax.rem(z + k - 1, nz)]
            put(piece, piece, down_sem.at[s, k - 1], "dp", below)

    def gather_event(s, k):
        if k == 0:
            wait_piece(s)
        else:
            if k <= ups:
                got(wbuf.at[s, lax.rem(z - k + nz, nz)], up_sem.at[s, k - 1])
            if k <= downs:
                got(wbuf.at[s, lax.rem(z + k, nz)], down_sem.at[s, k - 1])
        gather_send(s, k + 1)

    events = sorted((k + LAG * s, s, k) for s in range(sections) for k in range(ups + 1))

    def gather_until(key):
        while events and events[0][0] <= key:
            _, s, k = events.pop(0)
            gather_event(s, k)

    gather_until(0)

    lane = lax.broadcasted_iota(jnp.int32, (own, LANES), 1)

    micro, cap = inputs.shape[0], inputs.shape[1]
    slot = lax.broadcasted_iota(jnp.int32, (cap, LANES), 1)
    row = lax.broadcasted_iota(jnp.int32, (cap, LANES), 0)
    first = jnp.int32(0)
    factor = jnp.zeros((own, LANES), F32)
    start_block = jnp.zeros((width, LANES), F32)
    target_block = jnp.zeros((width, LANES), F32)
    over_rows = (((0,), (0,)), ((), ()))
    for m in range(micro):
        count = lengths[0, m]
        chosen = jnp.where((slot - row == first) & (row < count), 1.0, 0.0).astype(BF16)
        start_block += lax.dot_general(inputs[m], chosen, over_rows, preferred_element_type=F32)
        target_block += lax.dot_general(velocity[m], chosen, over_rows, preferred_element_type=F32)
        step = jnp.broadcast_to(steps[0, m], (own, LANES)).astype(F32)
        weighting = 1.0 / (0.1 + (step + 0.5) / NSTEPS)
        inside = (lane >= first) & (lane < first + count)
        factor = jnp.where(inside, weighting / math.sqrt(LIVE_PER_CLIP * nz), factor)
        first = first + count
    picked[0] = start_block.astype(BF16).reshape(HALVES * nx, chunk, LANES)
    picked[1] = target_block.astype(BF16).reshape(HALVES * nx, chunk, LANES)

    def own_part(which):
        return jnp.concatenate([picked[which, half * nx + x] for half in range(HALVES)], axis=0)

    abuf[0, t] = own_part(0)

    def a_sends(s):
        for d in range(1, nt):
            put(abuf.at[s, t], abuf.at[s, t], a_sem.at[s, t], "tensor", lax.rem(t + d, nt))

    a_sends(0)
    gather_until(1)

    for d in range(1, nx):
        at = lax.rem(x + d, nx)
        got(small.at[pl.ds(pl.multiple_of(at * SMALL_ROWS, 8), SMALL_ROWS)], small_sem.at[at])
    columns = jnp.transpose(small[...])
    wide_lane = lax.broadcasted_iota(jnp.int32, (chunk, LANES), 1)

    def spread_gains(s):
        for unit in range(nz):
            at = s * SMALL_ROWS + unit
            part = jnp.broadcast_to(columns[0:chunk, at:at + 1], (chunk, LANES))
            gainb[s, unit * chunk:(unit + 1) * chunk] = part
            a, b, c = (p.astype(F32) for p in split3(part))
            tail = jnp.where(wide_lane == PARTS_AT + 1, a, 0.0)
            tail = jnp.where(wide_lane == PARTS_AT + 2, b, tail)
            tail = jnp.where(wide_lane == PARTS_AT + 3, c, tail)
            gtail[s, unit * chunk:(unit + 1) * chunk] = tail
        for half in range(HALVES):
            at = s * SMALL_ROWS + 16 + half
            part = jnp.broadcast_to(columns[0:chunk, at:at + 1], (chunk, LANES))
            gateb[s, half * chunk:(half + 1) * chunk] = part

    for s in range(sections):
        spread_gains(s)
        gather_until(2 + s)

    factor = jnp.where(lane < LIVE_PER_CLIP, factor, 0.0)

    coeff = math.sqrt(2.0 / math.pi)
    state = None
    for s in range(sections):
        if s > 0:
            abuf[s, t] = state
            a_sends(s)
        gather_until(ups + LAG * s)
        weight = wbuf[s].reshape(deep, width)
        wt[...] = jnp.transpose(weight)
        for d in range(1, nt):
            at = lax.rem(t + d, nt)
            got(abuf.at[s, at], a_sem.at[s, at])
        values = abuf[s].reshape(deep, LANES).astype(F32)
        slice_mean = jnp.sum(values, axis=0, keepdims=True) * (1.0 / deep)
        centred = values - slice_mean
        slice_square = jnp.sum(centred * centred, axis=0, keepdims=True)
        operand = (centred * gainb[s] + gtail[s]).astype(BF16)
        partial = jnp.dot(wt[...], operand, preferred_element_type=F32)
        rounding = partial - partial.astype(BF16).astype(F32)
        all_lane = lax.broadcasted_iota(jnp.int32, (width, LANES), 1)
        partial = jnp.where(
            all_lane == PARTS_AT, pltpu.roll(rounding, LANES - 1, 1), partial
        ).astype(BF16)
        stats = stat_rows(slice_mean, slice_square)
        for to in range(nx):
            for half in range(HALVES):
                at = half * (width // HALVES) + to * chunk
                bsend[s, to, half * chunk:(half + 1) * chunk] = partial[at:at + chunk]
            bsend[s, to, own:own + TAIL] = stats
        for d in range(1, nx):
            to = lax.rem(x + d, nx)
            put(bsend.at[s, to], bbuf.at[s, x], b_sem.at[s, x], "section", to)
        bbuf[s, x] = bsend[s, x]
        gather_until(ups + LAG * s + LAG - 1)
        for d in range(1, nx):
            at = lax.rem(x + d, nx)
            got(bbuf.at[s, at], b_sem.at[s, at])
        summed = jnp.zeros((own, LANES), F32)
        means, squares, sums = [], [], []
        for at in range(nx):
            block = bbuf[s, at, 0:own].astype(F32)
            summed += block
            sums.append(
                jnp.sum(jnp.where(lane >= PARTS_AT, block, 0.0), axis=1, keepdims=True)
            )
            one, two = joined(bbuf[s, at, own:own + TAIL])
            means.append(one)
            squares.append(two)
        mean = sum(means[1:], means[0]) * (1.0 / nx)
        square = sum(squares[1:], squares[0])
        for at in range(nx):
            square += deep * (means[at] - mean) * (means[at] - mean)
        inverse = lax.rsqrt(square * (1.0 / model) + EPS)
        total = jnp.where(lane < PARTS_AT, summed, 0.0)
        for at in range(nx):
            total += (means[at] - mean) * sums[at]
        v = total * inverse
        tanh = jnp.tanh(coeff * (v + 0.044715 * v * v * v))
        gelu = 0.5 * v * (1.0 + tanh)
        slope = 0.5 * (1.0 + tanh) + 0.5 * v * (1.0 - tanh * tanh) * coeff * (
            1.0 + 3.0 * 0.044715 * v * v
        )
        gate = gateb[s]
        projb[s] = v
        gelub[s] = gelu
        slopeb[s] = gate * slope
        meanb[s] = mean
        invb[s] = inverse
        ub[s] = jnp.broadcast_to(sum(sums[1:], sums[0]), (own, LANES))
        state = (abuf[s, t].astype(F32) + gate * gelu).astype(BF16)

    gather_until(ups + LAG * sections)

    target = own_part(1).astype(F32)
    upstream = (factor * (state.astype(F32) - target)).astype(BF16).astype(F32)
    vacc[...] = jnp.zeros_like(vacc)

    def scatter_send(s, k):
        if k <= ups:
            src = dwbuf.at[s, lax.rem(z + ups, nz)] if k == 1 else rs_up.at[s, k - 2]
            put(src, rs_up.at[s, k - 1], rsu_sem.at[s, k - 1], "dp", above)
        if k <= downs:
            src = dwbuf.at[s, lax.rem(z + nz - downs, nz)] if k == 1 else rs_down.at[s, k - 2]
            put(src, rs_down.at[s, k - 1], rsd_sem.at[s, k - 1], "dp", below)

    def scatter_event(s, k):
        if k == 0:
            scatter_send(s, 1)
            return
        if k <= ups:
            got(rs_up.at[s, k - 1], rsu_sem.at[s, k - 1])
        if k <= downs:
            got(rs_down.at[s, k - 1], rsd_sem.at[s, k - 1])
        if k < ups:
            mine = dwbuf[s, lax.rem(z + ups - k, nz)].astype(F32)
            rs_up[s, k - 1] = (rs_up[s, k - 1].astype(F32) + mine).astype(BF16)
        if k < downs:
            mine = dwbuf[s, lax.rem(z + nz - downs + k, nz)].astype(F32)
            rs_down[s, k - 1] = (rs_down[s, k - 1].astype(F32) + mine).astype(BF16)
        scatter_send(s, k + 1)
        if k == ups:
            whole = dwbuf[s, z].astype(F32) + rs_up[s, ups - 1].astype(F32)
            if downs > 0:
                whole = whole + rs_down[s, downs - 1].astype(F32)
            gw_send[s] = whole.astype(BF16)

            @pl.when(x != s)
            def _():
                put_to(gw_send.at[s], gw_in.at[x], gw_sem.at[x], s)

            @pl.when(x == s)
            def _():
                gw_in[x] = gw_send[s]

    def put_to(src, dst, recv, s):
        pltpu.make_async_remote_copy(
            src_ref=src, dst_ref=dst, send_sem=local_sem.at[1 + s], recv_sem=recv,
            device_id={"section": s}, device_id_type=MESH,
        ).start()

    back = sorted(
        (k + LAG * (sections - 1 - s), s, k) for s in range(sections) for k in range(ups + 1)
    )

    def scatter_until(key):
        while back and back[0][0] <= key:
            _, s, k = back.pop(0)
            scatter_event(s, k)

    for turn, s in enumerate(reversed(range(sections))):
        vacc[0:own] = jnp.where(
            lane == 2 * s, jnp.sum(upstream * gelub[s], axis=1, keepdims=True), vacc[0:own]
        )
        dproj = (upstream * slopeb[s]).astype(BF16)
        exact = dproj.astype(F32)
        first_part = jnp.sum(exact * ub[s], axis=0, keepdims=True)
        second_part = jnp.sum(exact * projb[s], axis=0, keepdims=True)
        dbuf[s, x, 0:own] = dproj
        dbuf[s, x, own:own + TAIL] = stat_rows(first_part, second_part)
        for d in range(1, nx):
            put(dbuf.at[s, x], dbuf.at[s, x], d_sem.at[s, x], "section", lax.rem(x + d, nx))
        if turn > 0:
            scatter_until(LAG * turn - 2)
        mean, inverse = meanb[s], invb[s]
        normed = (
            (abuf[s].reshape(deep, LANES).astype(F32) - mean) * inverse * gainb[s]
        ).astype(BF16)
        for d in range(1, nx):
            at = lax.rem(x + d, nx)
            got(dbuf.at[s, at], d_sem.at[s, at])
        whole = jnp.concatenate(
            [dbuf[s, at, half * chunk:(half + 1) * chunk] for half in range(HALVES) for at in range(nx)],
            axis=0,
        )
        first_sum = jnp.zeros((1, LANES), F32)
        second_sum = jnp.zeros((1, LANES), F32)
        for at in range(nx):
            one, two = joined(dbuf[s, at, own:own + TAIL])
            first_sum += one
            second_sum += two
        product = jnp.dot(wbuf[s].reshape(deep, width), whole, preferred_element_type=F32).astype(BF16)
        stats = stat_rows(first_sum, second_sum)
        for to in range(nt):
            qsend[s, to, 0:own] = product[to * own:(to + 1) * own]
            qsend[s, to, own:own + TAIL] = stats
        for d in range(1, nt):
            to = lax.rem(t + d, nt)
            put(qsend.at[s, to], qbuf.at[s, t], q_sem.at[s, t], "tensor", to)
        qbuf[s, t] = qsend[s, t]
        term = lax.dot_general(
            normed, whole, (((1,), (1,)), ((), ())), preferred_element_type=F32
        )
        dwbuf[s] = term.astype(BF16).reshape(nz, chunk, width)
        scatter_until(LAG * turn)
        for d in range(1, nt):
            at = lax.rem(t + d, nt)
            got(qbuf.at[s, at], q_sem.at[s, at])
        dnormed = jnp.zeros((own, LANES), F32)
        first_moment = jnp.zeros((1, LANES), F32)
        second_moment = jnp.zeros((1, LANES), F32)
        for at in range(nt):
            dnormed += qbuf[s, at, 0:own].astype(F32)
            one, two = joined(qbuf[s, at, own:own + TAIL])
            first_moment += one
            second_moment += two
        xhat = (abuf[s, t].astype(F32) - mean) * inverse
        vacc[0:own] = jnp.where(
            lane == 2 * s + 1, jnp.sum(dnormed * xhat, axis=1, keepdims=True), vacc[0:own]
        )
        if s > 0:
            gain = gainb[s, pl.ds(pl.multiple_of(t * own, 8), own)]
            change = dnormed * gain - first_moment * (1.0 / model) - xhat * (
                second_moment * (1.0 / model)
            )
            upstream = (upstream + inverse * change).astype(BF16).astype(F32)

    v1[member] = jnp.transpose(vacc[...])[0:8]
    for d in range(1, zb):
        to = group * zb + lax.rem(member + d, zb)
        put(v1.at[member], v1.at[member], v1_sem.at[member], "dp", to)
    scatter_until(LAG * sections - 1)
    for d in range(1, zb):
        at = lax.rem(member + d, zb)
        got(v1.at[at], v1_sem.at[at])
    v2[group] = v1[0] + v1[1] + v1[2] + v1[3]
    for d in range(1, za):
        to = lax.rem(group + d, za) * zb + member
        put(v2.at[group], v2.at[group], v2_sem.at[group], "dp", to)
    scatter_until(LAG * sections)
    for d in range(1, za):
        at = lax.rem(group + d, za)
        got(v2.at[at], v2_sem.at[at])
    full = v2[0]
    for at in range(1, za):
        full = full + v2[at]
    v3[x] = full
    for d in range(1, nx):
        put(v3.at[x], v3.at[x], v3_sem.at[x], "section", lax.rem(x + d, nx))
    scatter_until(LAG * sections + ups)
    for d in range(1, nx):
        at = lax.rem(x + d, nx)
        got(v3.at[at], v3_sem.at[at])
    for at in range(nx):
        tile = v3[at]
        gate_row, gain_row = tile[0:1], tile[1:2]
        for s in range(1, sections):
            gate_row = jnp.where(x == s, tile[2 * s:2 * s + 1], gate_row)
            gain_row = jnp.where(x == s, tile[2 * s + 1:2 * s + 2], gain_row)
        for half in range(HALVES):
            to = half * (width // HALVES) + at * chunk
            gate_out[0:1, to:to + chunk] = gate_row[:, half * chunk:(half + 1) * chunk]
            gain_out[0:1, to:to + chunk] = gain_row[:, half * chunk:(half + 1) * chunk]
    for d in range(1, nx):
        at = lax.rem(x + d, nx)
        got(gw_in.at[at], gw_sem.at[at])
    for at in range(nx):
        gw_out[0, at * chunk:(at + 1) * chunk] = gw_in[at].astype(F32)

    for copy in sends:
        copy.wait_send()
    for s in range(sections):
        @pl.when(x != s)
        def _():
            pltpu.make_async_remote_copy(
                src_ref=gw_send.at[s], dst_ref=gw_in.at[x], send_sem=local_sem.at[1 + s],
                recv_sem=gw_sem.at[x], device_id={"section": s}, device_id_type=MESH,
            ).wait_send()


def local(inputs, velocity, weights, gains, gates, lengths, steps):
    nx, nt, nz = lax.axis_size("section"), lax.axis_size("tensor"), lax.axis_size("dp")
    sections = nx
    width = inputs.shape[2]
    chunk = width // (HALVES * nx)
    own = HALVES * chunk
    deep = nt * own
    ups, downs = nz // 2, nz // 2 - 1
    block = own + TAIL
    sends = (
        2 * (nx - 1) + 2 * sections * (ups + downs) + 2 * sections * (nt - 1)
        + 2 * sections * (nx - 1) + 3 + nz // 4 - 1 + nx - 1
    )
    dma = pltpu.SemaphoreType.DMA
    vmem = pl.BlockSpec(memory_space=pltpu.VMEM)
    smem = pl.BlockSpec(memory_space=pltpu.SMEM)
    return pl.pallas_call(
        functools.partial(kernel, nx, nt, nz),
        out_shape=(
            jax.ShapeDtypeStruct((1, nx * chunk, width), F32),
            jax.ShapeDtypeStruct((1, width), F32),
            jax.ShapeDtypeStruct((1, width), F32),
        ),
        in_specs=[vmem, vmem, vmem, vmem, vmem, smem, smem],
        out_specs=(vmem, vmem, vmem),
        scratch_shapes=[
            pltpu.VMEM((sections, nz, chunk, width), BF16),
            pltpu.VMEM((width, deep), BF16),
            pltpu.VMEM((nx, SMALL_ROWS, LANES), F32),
            pltpu.VMEM((LANES, LANES), F32),
            pltpu.VMEM((sections, deep, LANES), F32),
            pltpu.VMEM((sections, deep, LANES), F32),
            pltpu.VMEM((sections, own, LANES), F32),
            pltpu.VMEM((2, HALVES * nx, chunk, LANES), BF16),
            pltpu.VMEM((sections, nt, own, LANES), BF16),
            pltpu.VMEM((sections, nx, block, LANES), BF16),
            pltpu.VMEM((sections, nx, block, LANES), BF16),
            pltpu.VMEM((sections, own, LANES), F32),
            pltpu.VMEM((sections, own, LANES), F32),
            pltpu.VMEM((sections, own, LANES), F32),
            pltpu.VMEM((sections, 1, LANES), F32),
            pltpu.VMEM((sections, 1, LANES), F32),
            pltpu.VMEM((sections, own, LANES), F32),
            pltpu.VMEM((sections, nx, block, LANES), BF16),
            pltpu.VMEM((sections, nt, block, LANES), BF16),
            pltpu.VMEM((sections, nt, block, LANES), BF16),
            pltpu.VMEM((sections, nz, chunk, width), BF16),
            pltpu.VMEM((sections, ups, chunk, width), BF16),
            pltpu.VMEM((sections, max(downs, 1), chunk, width), BF16),
            pltpu.VMEM((sections, chunk, width), BF16),
            pltpu.VMEM((nx, chunk, width), BF16),
            pltpu.VMEM((LANES, LANES), F32),
            pltpu.VMEM((4, 8, LANES), F32),
            pltpu.VMEM((max(nz // 4, 1), 8, LANES), F32),
            pltpu.VMEM((nx, 8, LANES), F32),
            dma((sends,)),
            dma((1 + sections,)),
            dma((nx,)),
            dma((nx,)),
            dma((sections, ups)),
            dma((sections, max(downs, 1))),
            dma((sections, nt)),
            dma((sections, nx)),
            dma((sections, nx)),
            dma((sections, nt)),
            dma((sections, ups)),
            dma((sections, max(downs, 1))),
            dma((nx,)),
            dma((4,)),
            dma((max(nz // 4, 1),)),
            dma((nx,)),
        ],
        compiler_params=pltpu.CompilerParams(
            collective_id=0, has_side_effects=True, vmem_limit_bytes=48 * 1024 * 1024
        ),
        name="sections",
    )(weights, inputs, velocity, gains, gates, lengths, steps)


def solution(mesh):
    placed = (
        P(None, "dp", "tensor"),
        P(None, "dp", "tensor"),
        P("section", "dp", "tensor"),
        P("section", None),
        P("section", "tensor"),
        P("dp", None),
        P("dp", None),
    )

    def whole(*args):
        return jax.shard_map(
            local, mesh=mesh, in_specs=placed,
            out_specs=(P("section", "dp", "tensor"), P("section", "tensor"), P("section", "tensor")),
            check_vma=False,
        )(*args)

    return whole
```

time: 887 us -> 171 us (0.19)
  waiting for transfers between devices: 622 us -> 0 us
  Pallas kernels: 0 us -> 163 us
  blocking collectives: 124 us -> 0 us
  matrix products: 51.1 us -> 0 us
  starting transfers between devices: 33.2 us -> 0 us
  other arithmetic: 31.9 us -> 0 us
  between operations: 14.7 us -> 0.66 us
    psum x7 -> x0, waiting for transfers between devices: 495 us -> none  [local(): lax.psum(partial_value.astype(jnp.bfloat16), 'tensor').astype(jnp.float32)]
    pallas_call x0 -> x1, Pallas kernels: none -> 163 us  [local(): pl.pallas_call(functools.partial(kernel, nx, nt, nz), out_shape=(jax.Shap...]
    all_gather x7 -> x0, blocking collectives: 92.4 us -> none  [local(): lax.all_gather(arriving_input, 'tensor', axis=1, tiled=True)]
    all_gather x1 -> x0, waiting for transfers between devices: 57.8 us -> none  [local(): full_weight = lax.all_gather(proj_weights[0], 'dp', axis=0, tiled=True)]
    dot_general x21 -> x0, matrix products: 51.1 us -> none  [the longest x7 33.3 us: local(): lax.dot_general(normed_rows, dproj, (((0,), (0,)), ((), ())), preferred_e...]
    reduce_scatter x1 -> x0, waiting for transfers between devices: 47 us -> none  [local(): lax.psum_scatter(weight_acc.astype(jnp.bfloat16), 'dp', scatter_dimension...]
    ppermute x12 -> x0, starting transfers between devices: 32.4 us -> none  [passed_along(): return lax.ppermute(block, axis, route)]
    psum x1 -> x0, blocking collectives: 31.8 us -> none  [local(): gate_sum, gain_sum = lax.psum((gate_acc, gain_accumulator), 'dp')]
  transfers between devices with their start and end apart: 21 -> 0, of which waited for: 21 -> 0; matrix products, arithmetic and copies ran while one was open for 5% -> 0% of each run, Pallas kernels for 0% -> 0%
where the time goes in v1:
time: 171 us
  Pallas kernels  163 us (95%)
  local copies, waits for them, and re-layouts  7.24 us (4%)
    pallas_call x1, Pallas kernels, local(): pl.pallas_call(functools.partial(kernel, nx, nt, nz), out_shape=(jax.Shap...  163 us
    unnamed x17, local copies, waits for them, and re-layouts  7.24 us

profile of v1, /device:TPU:16, one launch (start us, length us, event | category | flops | bytes accessed | tf_op | source)
XLA Modules:
  0.0 170.5 jit_solution(4301334582921438311)
XLA Ops:
  0.6 0.0 copy-start
  0.6 0.9 copy-done
  1.5 0.0 copy-start.1
  1.5 0.9 copy-done.1
  2.4 0.0 copy-start.2
  2.4 0.9 copy-done.2
  3.3 0.0 copy-start.3
  3.4 0.7 copy-done.3
  4.1 0.0 copy-start.4
  4.1 0.7 copy-done.4
  4.7 0.0 copy-start.5
  4.7 0.7 copy-done.5
  5.4 0.0 copy-start.6
  5.4 0.7 copy-done.6
  6.0 162.6 %sections.1 = (f32[1,192,384]{2,1,0:T(8,128)S(1)}, f32[1,384]{1,0:T(1,128)S(1)}, f32[1,384]{1,0:T(1,128)S(1)}) custom-call(bf16[1,192,384]{2,1,0:T(8,128)(2,1)S(1)} %copy-done, bf16[4,40,384]{2,1,0:T(8,128)(2,1)S(1)} %copy-done.1, bf16[4,40,384]{2,1,0:T(8,128)(2,1)S(1)} %copy-done.2, f32[1,3072]{1,0:T(1,128)S(1)} %copy-done.3, f32[1,384]{1,0:T(1,128)S(1)} %copy-done.4, ...), custom_call_target="tpu_custom_call" | custom-call | tf_op jit(solution)/shard_map/sections/pallas_call | solution.py:495
  168.7 0.7 copy.13
  169.4 0.6 copy.14
  170.0 0.6 copy.15
Async XLA Ops:
  0.6 0.9 copy-start
  1.5 0.9 copy-start.1
  2.4 0.9 copy-start.2
  3.3 0.7 copy-start.3
  4.1 0.7 copy-start.4
  4.7 0.7 copy-start.5
  5.4 0.7 copy-start.6

commit v2 on v1

--- a/solution.py
+++ b/solution.py
@@ -19,7 +19,9 @@
 SMALL_ROWS = 24
 TAIL = 16
 PARTS_AT = 124
-LAG = 3
+LAG = 2
+GATHER_REACH = (2, 2, 2, 2)
+SCATTER_REACH = (2, 2, 2, 2)
 
 
 def split3(value):
@@ -45,12 +47,13 @@
 
 def kernel(
     nx, nt, nz,
-    w_in, inputs, velocity, gains, gates, lengths, steps,
+    w_in, inputs_in, velocity_in, gains_in, gates_in, lengths_in, steps_in,
     gw_out, gain_out, gate_out,
+    inputs, velocity, gains, gates, lengths, steps,
     wbuf, wt, small_src, small, gainb, gtail, gateb, picked, abuf, bsend, bbuf,
     projb, gelub, slopeb, meanb, invb, ub, dbuf, qsend, qbuf, dwbuf, rs_up, rs_down,
     gw_send, gw_in, vacc, v1, v2, v3,
-    send_sem, local_sem, w_sem, small_sem, up_sem, down_sem, a_sem, b_sem, d_sem, q_sem,
+    send_sem, local_sem, load_sem, w_sem, small_sem, up_sem, down_sem, a_sem, b_sem, d_sem, q_sem,
     rsu_sem, rsd_sem, gw_sem, v1_sem, v2_sem, v3_sem,
 ):
     sections = nx
@@ -66,7 +69,6 @@
     t = lax.axis_index("tensor")
     z = lax.axis_index("dp")
     above = lax.rem(z + 1, nz)
-    below = lax.rem(z + nz - 1, nz)
     group, member = z // zb, lax.rem(z, zb)
 
     small[...] = jnp.zeros_like(small)
@@ -79,9 +81,11 @@
     for d in range(1, nx):
         greet("section", lax.rem(x + d, nx))
         greeted += 1
-    greet("dp", above)
-    greet("dp", below)
-    greeted += 2
+    far = max(GATHER_REACH + SCATTER_REACH)
+    for d in range(1, far + 1):
+        greet("dp", lax.rem(z + d, nz))
+        greet("dp", lax.rem(z + nz - d, nz))
+        greeted += 2
     for d in range(1, nt):
         greet("tensor", lax.rem(t + d, nt))
         greeted += 1
@@ -108,10 +112,21 @@
             device_id={"dp": above}, device_id_type=MESH,
         ).wait_recv()
 
+    loads = [
+        pltpu.make_async_copy(src, dst, load_sem.at[i])
+        for i, (src, dst) in enumerate((
+            (gains_in, gains), (gates_in, gates), (inputs_in, inputs), (velocity_in, velocity),
+            (lengths_in, lengths), (steps_in, steps),
+        ))
+    ]
+    for load in loads:
+        load.start()
     own_rows = pl.ds(pl.multiple_of(x * chunk, 16), chunk)
     keep = pltpu.make_async_copy(w_in.at[0, own_rows], wbuf.at[x, z], local_sem.at[0])
     keep.start()
     small_src[...] = jnp.zeros_like(small_src)
+    for load in loads:
+        load.wait()
     for to in range(nx):
         for unit in range(nz):
             at = unit * (width // HALVES) + to * chunk
@@ -138,30 +153,41 @@
         def _():
             got(wbuf.at[s, z], w_sem.at[s])
 
-    def gather_send(s, k):
-        if k <= ups:
-            piece = wbuf.at[s, lax.rem(z - k + 1 + nz, nz)]
-            put(piece, piece, up_sem.at[s, k - 1], "dp", above)
-        if k <= downs:
-            piece = wbuf.at[s, lax.rem(z + k - 1, nz)]
-            put(piece, piece, down_sem.at[s, k - 1], "dp", below)
-
-    def gather_event(s, k):
-        if k == 0:
+    def stages(reach):
+        return -(-ups // reach)
+
+    def gather_event(s, j):
+        reach = GATHER_REACH[s]
+        if j == 0:
             wait_piece(s)
-        else:
-            if k <= ups:
-                got(wbuf.at[s, lax.rem(z - k + nz, nz)], up_sem.at[s, k - 1])
-            if k <= downs:
-                got(wbuf.at[s, lax.rem(z + k, nz)], down_sem.at[s, k - 1])
-        gather_send(s, k + 1)
-
-    events = sorted((k + LAG * s, s, k) for s in range(sections) for k in range(ups + 1))
+        for way, total, sem in ((1, ups, up_sem), (-1, downs, down_sem)):
+            gone = j * reach
+            if j == stages(reach):
+                for q in range(1, total + 1):
+                    if q % reach or q >= total:
+                        got(wbuf.at[s, lax.rem(z - way * q + nz, nz)], sem.at[s, q - 1])
+                continue
+            if gone >= total:
+                continue
+            piece = wbuf.at[s, lax.rem(z - way * gone + nz, nz)]
+            if j > 0:
+                got(piece, sem.at[s, gone - 1])
+            for d in range(min(reach, total - gone), 0, -1):
+                put(piece, piece, sem.at[s, gone + d - 1], "dp", lax.rem(z + way * d + nz, nz))
+
+    events = sorted(
+        (j + LAG * s, s, j) for s in range(sections) for j in range(stages(GATHER_REACH[s]) + 1)
+    )
 
     def gather_until(key):
         while events and events[0][0] <= key:
-            _, s, k = events.pop(0)
-            gather_event(s, k)
+            _, s, j = events.pop(0)
+            gather_event(s, j)
+
+    def gather_all_of(s):
+        while any(event[1] == s for event in events):
+            _, section, j = events.pop(0)
+            gather_event(section, j)
 
     gather_until(0)
 
@@ -170,17 +196,17 @@
     micro, cap = inputs.shape[0], inputs.shape[1]
     slot = lax.broadcasted_iota(jnp.int32, (cap, LANES), 1)
     row = lax.broadcasted_iota(jnp.int32, (cap, LANES), 0)
-    first = jnp.int32(0)
+    first = jnp.zeros((1, 1), jnp.int32)
     factor = jnp.zeros((own, LANES), F32)
     start_block = jnp.zeros((width, LANES), F32)
     target_block = jnp.zeros((width, LANES), F32)
     over_rows = (((0,), (0,)), ((), ()))
     for m in range(micro):
-        count = lengths[0, m]
+        count = lengths[0:1, m:m + 1]
         chosen = jnp.where((slot - row == first) & (row < count), 1.0, 0.0).astype(BF16)
         start_block += lax.dot_general(inputs[m], chosen, over_rows, preferred_element_type=F32)
         target_block += lax.dot_general(velocity[m], chosen, over_rows, preferred_element_type=F32)
-        step = jnp.broadcast_to(steps[0, m], (own, LANES)).astype(F32)
+        step = jnp.broadcast_to(steps[0:1, m:m + 1], (own, LANES)).astype(F32)
         weighting = 1.0 / (0.1 + (step + 0.5) / NSTEPS)
         inside = (lane >= first) & (lane < first + count)
         factor = jnp.where(inside, weighting / math.sqrt(LIVE_PER_CLIP * nz), factor)
@@ -223,9 +249,13 @@
 
     for s in range(sections):
         spread_gains(s)
-        gather_until(2 + s)
+        if s < 2:
+            gather_until(2)
 
     factor = jnp.where(lane < LIVE_PER_CLIP, factor, 0.0)
+
+    def key_after(s):
+        return stages(2) + LAG * s + 1
 
     coeff = math.sqrt(2.0 / math.pi)
     state = None
@@ -233,7 +263,7 @@
         if s > 0:
             abuf[s, t] = state
             a_sends(s)
-        gather_until(ups + LAG * s)
+        gather_all_of(s)
         weight = wbuf[s].reshape(deep, width)
         wt[...] = jnp.transpose(weight)
         for d in range(1, nt):
@@ -260,7 +290,7 @@
             to = lax.rem(x + d, nx)
             put(bsend.at[s, to], bbuf.at[s, x], b_sem.at[s, x], "section", to)
         bbuf[s, x] = bsend[s, x]
-        gather_until(ups + LAG * s + LAG - 1)
+        gather_until(key_after(s))
         for d in range(1, nx):
             at = lax.rem(x + d, nx)
             got(bbuf.at[s, at], b_sem.at[s, at])
@@ -298,40 +328,40 @@
         ub[s] = jnp.broadcast_to(sum(sums[1:], sums[0]), (own, LANES))
         state = (abuf[s, t].astype(F32) + gate * gelu).astype(BF16)
 
-    gather_until(ups + LAG * sections)
 
     target = own_part(1).astype(F32)
     upstream = (factor * (state.astype(F32) - target)).astype(BF16).astype(F32)
     vacc[...] = jnp.zeros_like(vacc)
 
-    def scatter_send(s, k):
-        if k <= ups:
-            src = dwbuf.at[s, lax.rem(z + ups, nz)] if k == 1 else rs_up.at[s, k - 2]
-            put(src, rs_up.at[s, k - 1], rsu_sem.at[s, k - 1], "dp", above)
-        if k <= downs:
-            src = dwbuf.at[s, lax.rem(z + nz - downs, nz)] if k == 1 else rs_down.at[s, k - 2]
-            put(src, rs_down.at[s, k - 1], rsd_sem.at[s, k - 1], "dp", below)
-
-    def scatter_event(s, k):
-        if k == 0:
-            scatter_send(s, 1)
-            return
-        if k <= ups:
-            got(rs_up.at[s, k - 1], rsu_sem.at[s, k - 1])
-        if k <= downs:
-            got(rs_down.at[s, k - 1], rsd_sem.at[s, k - 1])
-        if k < ups:
-            mine = dwbuf[s, lax.rem(z + ups - k, nz)].astype(F32)
-            rs_up[s, k - 1] = (rs_up[s, k - 1].astype(F32) + mine).astype(BF16)
-        if k < downs:
-            mine = dwbuf[s, lax.rem(z + nz - downs + k, nz)].astype(F32)
-            rs_down[s, k - 1] = (rs_down[s, k - 1].astype(F32) + mine).astype(BF16)
-        scatter_send(s, k + 1)
-        if k == ups:
-            whole = dwbuf[s, z].astype(F32) + rs_up[s, ups - 1].astype(F32)
-            if downs > 0:
-                whole = whole + rs_down[s, downs - 1].astype(F32)
-            gw_send[s] = whole.astype(BF16)
+    def scatter_event(s, turn):
+        reach = SCATTER_REACH[s]
+        relay = stages(reach) - turn
+        mine = dwbuf[s, z].astype(F32) if relay == 0 else None
+        for way, total, slots, sem in ((1, ups, rs_up, rsu_sem), (-1, downs, rs_down, rsd_sem)):
+            if turn == 0:
+                for q in range(total, 0, -1):
+                    if q % reach and q > 0 or q == total:
+                        d = q - reach * ((q - 1) // reach)
+                        to = lax.rem(z + way * d + nz, nz)
+                        term = dwbuf.at[s, lax.rem(z + way * q + nz, nz)]
+                        put(term, slots.at[s, q - 1], sem.at[s, q - 1], "dp", to)
+                continue
+            gone = relay * reach
+            if gone >= total:
+                continue
+            children = range(gone + 1, min(gone + reach, total) + 1)
+            for q in children:
+                got(slots.at[s, q - 1], sem.at[s, q - 1])
+            if relay > 0:
+                mine = dwbuf[s, lax.rem(z + way * gone + nz, nz)].astype(F32)
+            for q in children:
+                mine = mine + slots[s, q - 1].astype(F32)
+            if relay > 0:
+                slots[s, gone] = mine.astype(BF16)
+                to = lax.rem(z + way * reach + nz, nz)
+                put(slots.at[s, gone], slots.at[s, gone - 1], sem.at[s, gone - 1], "dp", to)
+        if relay == 0:
+            gw_send[s] = mine.astype(BF16)
 
             @pl.when(x != s)
             def _():
@@ -348,13 +378,14 @@
         ).start()
 
     back = sorted(
-        (k + LAG * (sections - 1 - s), s, k) for s in range(sections) for k in range(ups + 1)
+        (turn + LAG * (sections - 1 - s), s, turn)
+        for s in range(sections) for turn in range(stages(SCATTER_REACH[s]) + 1)
     )
 
     def scatter_until(key):
         while back and back[0][0] <= key:
-            _, s, k = back.pop(0)
-            scatter_event(s, k)
+            _, s, turn = back.pop(0)
+            scatter_event(s, turn)
 
     for turn, s in enumerate(reversed(range(sections))):
         vacc[0:own] = jnp.where(
@@ -369,7 +400,7 @@
         for d in range(1, nx):
             put(dbuf.at[s, x], dbuf.at[s, x], d_sem.at[s, x], "section", lax.rem(x + d, nx))
         if turn > 0:
-            scatter_until(LAG * turn - 2)
+            scatter_until(LAG * turn - 1)
         mean, inverse = meanb[s], invb[s]
         normed = (
             (abuf[s].reshape(deep, LANES).astype(F32) - mean) * inverse * gainb[s]
@@ -427,7 +458,7 @@
     for d in range(1, zb):
         to = group * zb + lax.rem(member + d, zb)
         put(v1.at[member], v1.at[member], v1_sem.at[member], "dp", to)
-    scatter_until(LAG * sections - 1)
+    scatter_until(LAG * (sections - 1) + 1)
     for d in range(1, zb):
         at = lax.rem(member + d, zb)
         got(v1.at[at], v1_sem.at[at])
@@ -435,7 +466,7 @@
     for d in range(1, za):
         to = lax.rem(group + d, za) * zb + member
         put(v2.at[group], v2.at[group], v2_sem.at[group], "dp", to)
-    scatter_until(LAG * sections)
+    scatter_until(LAG * (sections - 1) + 2)
     for d in range(1, za):
         at = lax.rem(group + d, za)
         got(v2.at[at], v2_sem.at[at])
@@ -491,7 +522,7 @@
     )
     dma = pltpu.SemaphoreType.DMA
     vmem = pl.BlockSpec(memory_space=pltpu.VMEM)
-    smem = pl.BlockSpec(memory_space=pltpu.SMEM)
+    anywhere = pl.BlockSpec(memory_space=pl.ANY)
     return pl.pallas_call(
         functools.partial(kernel, nx, nt, nz),
         out_shape=(
@@ -499,9 +530,15 @@
             jax.ShapeDtypeStruct((1, width), F32),
             jax.ShapeDtypeStruct((1, width), F32),
         ),
-        in_specs=[vmem, vmem, vmem, vmem, vmem, smem, smem],
+        in_specs=[anywhere] * 7,
         out_specs=(vmem, vmem, vmem),
         scratch_shapes=[
+            pltpu.VMEM(inputs.shape, BF16),
+            pltpu.VMEM(velocity.shape, BF16),
+            pltpu.VMEM(gains.shape, F32),
+            pltpu.VMEM(gates.shape, F32),
+            pltpu.VMEM(lengths.shape, jnp.int32),
+            pltpu.VMEM(steps.shape, jnp.int32),
             pltpu.VMEM((sections, nz, chunk, width), BF16),
             pltpu.VMEM((width, deep), BF16),
             pltpu.VMEM((nx, SMALL_ROWS, LANES), F32),
@@ -533,6 +570,7 @@
             pltpu.VMEM((nx, 8, LANES), F32),
             dma((sends,)),
             dma((1 + sections,)),
+            dma((6,)),
             dma((nx,)),
             dma((nx,)),
             dma((sections, ups)),

time: 171 us -> 147 us (0.86)
  the two profiles are of different devices: /device:TPU:16 before, /device:TPU:32 now
where the time goes in v2:
time: 147 us
  Pallas kernels  139 us (95%)
  local copies, waits for them, and re-layouts  7.24 us (5%)
    pallas_call x1, Pallas kernels, local(): pl.pallas_call(functools.partial(kernel, nx, nt, nz), out_shape=(jax.Shap...  139 us
    unnamed x17, local copies, waits for them, and re-layouts  7.24 us

profile of v2, /device:TPU:32, one launch (start us, length us, event | category | flops | bytes accessed | tf_op | source)
XLA Modules:
  0.0 147.1 jit_solution(13474557461287309954)
XLA Ops:
  0.6 0.0 copy-start
  0.6 0.9 copy-done
  1.5 0.0 copy-start.1
  1.5 0.9 copy-done.1
  2.4 0.0 copy-start.2
  2.4 0.9 copy-done.2
  3.3 0.0 copy-start.3
  3.4 0.7 copy-done.3
  4.1 0.0 copy-start.4
  4.1 0.7 copy-done.4
  4.7 0.0 copy-start.5
  4.7 0.7 copy-done.5
  5.4 0.0 copy-start.6
  5.4 0.7 copy-done.6
  6.0 139.2 %sections.1 = (f32[1,192,384]{2,1,0:T(8,128)S(1)}, f32[1,384]{1,0:T(1,128)S(1)}, f32[1,384]{1,0:T(1,128)S(1)}) custom-call(bf16[1,192,384]{2,1,0:T(8,128)(2,1)S(1)} %copy-done, bf16[4,40,384]{2,1,0:T(8,128)(2,1)S(1)} %copy-done.1, bf16[4,40,384]{2,1,0:T(8,128)(2,1)S(1)} %copy-done.2, f32[1,3072]{1,0:T(1,128)S(1)} %copy-done.3, f32[1,384]{1,0:T(1,128)S(1)} %copy-done.4, ...), custom_call_target="tpu_custom_call" | custom-call | tf_op jit(solution)/shard_map/sections/pallas_call | solution.py:526
  145.3 0.7 copy.13
  146.0 0.6 copy.14
  146.6 0.6 copy.15
Async XLA Ops:
  0.6 0.9 copy-start
  1.5 0.9 copy-start.1
  2.4 0.9 copy-start.2
  3.3 0.7 copy-start.3
  4.1 0.7 copy-start.4
  4.7 0.7 copy-start.5
  5.4 0.7 copy-start.6

commit v3 on v2

--- a/solution.py
+++ b/solution.py
@@ -88,12 +88,6 @@
         greeted += 2
     for d in range(1, nt):
         greet("tensor", lax.rem(t + d, nt))
-        greeted += 1
-    for d in range(1, zb):
-        greet("dp", group * zb + lax.rem(member + d, zb))
-        greeted += 1
-    for d in range(1, za):
-        greet("dp", lax.rem(group + d, za) * zb + member)
         greeted += 1
 
     sends = []
@@ -522,7 +516,7 @@
     )
     dma = pltpu.SemaphoreType.DMA
     vmem = pl.BlockSpec(memory_space=pltpu.VMEM)
-    anywhere = pl.BlockSpec(memory_space=pl.ANY)
+    anywhere = pl.BlockSpec(memory_space=pltpu.HBM)
     return pl.pallas_call(
         functools.partial(kernel, nx, nt, nz),
         out_shape=(
@@ -587,7 +581,7 @@
             dma((nx,)),
         ],
         compiler_params=pltpu.CompilerParams(
-            collective_id=0, has_side_effects=True, vmem_limit_bytes=48 * 1024 * 1024
+            collective_id=0, has_side_effects=True, vmem_limit_bytes=64 * 1024 * 1024
         ),
         name="sections",
     )(weights, inputs, velocity, gains, gates, lengths, steps)

time: 147 us -> 141 us (0.959)
  the two profiles are of different devices: /device:TPU:32 before, /device:TPU:16 now
where the time goes in v3:
time: 141 us
  Pallas kernels  137 us (97%)
  local copies, waits for them, and re-layouts  2.91 us (2%)
    pallas_call x1, Pallas kernels, local(): pl.pallas_call(functools.partial(kernel, nx, nt, nz), out_shape=(jax.Shap...  137 us
    unnamed x7, local copies, waits for them, and re-layouts  2.91 us

profile of v3, /device:TPU:16, one launch (start us, length us, event | category | flops | bytes accessed | tf_op | source)
XLA Modules:
  0.0 140.8 jit_solution(7734996215259479850)
XLA Ops:
  0.6 137.3 %sections.1 = (f32[1,192,384]{2,1,0:T(8,128)}, f32[1,384]{1,0:T(1,128)}, f32[1,384]{1,0:T(1,128)}) custom-call(bf16[1,192,384]{2,1,0:T(8,128)(2,1)} %w_in.1, bf16[4,40,384]{2,1,0:T(8,128)(2,1)} %inputs_in.1, bf16[4,40,384]{2,1,0:T(8,128)(2,1)} %velocity_in.1, f32[1,3072]{1,0:T(1,128)} %gains_in.1, f32[1,384]{1,0:T(1,128)} %gates_in.1, s32[1,4]{1,0:T(1,128)} %lengths_in.1, ...), custom_call_target="tpu_custom_call" | custom-call | tf_op jit(solution)/shard_map/sections/pallas_call | solution.py:520
  137.9 0.0 copy-start.1
  137.9 1.7 %copy.13 = f32[1,192,384]{2,1,0:T(8,128)} copy(f32[1,192,384]{2,1,0:T(8,128)} %get-tuple-element.6) | data formatting | bytes 589824
  139.6 0.0 copy-done.1
  139.6 0.0 copy-start
  139.6 0.6 copy.14
  140.2 0.1 copy-done
  140.3 0.6 copy.15
Async XLA Ops:
  137.9 1.7 %copy-start.1 = (f32[1,384]{1,0:T(1,128)S(1)}, f32[1,384]{1,0:T(1,128)}, u32[]{:S(2)}) copy-start(f32[1,384]{1,0:T(1,128)} %get-tuple-element.7) | copy-start | bytes 4612
  139.6 0.7 copy-start

commit v4 on v3

--- a/solution.py
+++ b/solution.py
@@ -19,9 +19,10 @@
 SMALL_ROWS = 24
 TAIL = 16
 PARTS_AT = 124
-LAG = 2
-GATHER_REACH = (2, 2, 2, 2)
+GATHER_REACH = (2, 2, 1, 1)
+GATHER_START = (0, 2, 0, 2)
 SCATTER_REACH = (2, 2, 2, 2)
+SCATTER_START = (6, 4, 2, 0)
 
 
 def split3(value):
@@ -48,7 +49,7 @@
 def kernel(
     nx, nt, nz,
     w_in, inputs_in, velocity_in, gains_in, gates_in, lengths_in, steps_in,
-    gw_out, gain_out, gate_out,
+    gw_part, row_part,
     inputs, velocity, gains, gates, lengths, steps,
     wbuf, wt, small_src, small, gainb, gtail, gateb, picked, abuf, bsend, bbuf,
     projb, gelub, slopeb, meanb, invb, ub, dbuf, qsend, qbuf, dwbuf, rs_up, rs_down,
@@ -90,6 +91,8 @@
         greet("tensor", lax.rem(t + d, nt))
         greeted += 1
 
+    far_x = sorted(range(1, nx), key=lambda d: -min(d, nx - d))
+    far_t = sorted(range(1, nt), key=lambda d: -min(d, nt - d))
     sends = []
 
     def put(src, dst, recv, axis, index):
@@ -131,7 +134,7 @@
 
     pl.semaphore_wait(barrier, greeted)
 
-    for d in range(1, nx):
+    for d in far_x:
         to = lax.rem(x + d, nx)
         rows = pl.ds(pl.multiple_of(to * chunk, 16), chunk)
         put(w_in.at[0, rows], wbuf.at[x, z], w_sem.at[x], "section", to)
@@ -170,7 +173,7 @@
                 put(piece, piece, sem.at[s, gone + d - 1], "dp", lax.rem(z + way * d + nz, nz))
 
     events = sorted(
-        (j + LAG * s, s, j) for s in range(sections) for j in range(stages(GATHER_REACH[s]) + 1)
+        (j + GATHER_START[s], s, j) for s in range(sections) for j in range(stages(GATHER_REACH[s]) + 1)
     )
 
     def gather_until(key):
@@ -214,7 +217,7 @@
     abuf[0, t] = own_part(0)
 
     def a_sends(s):
-        for d in range(1, nt):
+        for d in far_t:
             put(abuf.at[s, t], abuf.at[s, t], a_sem.at[s, t], "tensor", lax.rem(t + d, nt))
 
     a_sends(0)
@@ -244,12 +247,12 @@
     for s in range(sections):
         spread_gains(s)
         if s < 2:
-            gather_until(2)
+            gather_until(2 + s)
 
     factor = jnp.where(lane < LIVE_PER_CLIP, factor, 0.0)
 
     def key_after(s):
-        return stages(2) + LAG * s + 1
+        return stages(GATHER_REACH[0]) + 2 * s + 1
 
     coeff = math.sqrt(2.0 / math.pi)
     state = None
@@ -280,7 +283,7 @@
                 at = half * (width // HALVES) + to * chunk
                 bsend[s, to, half * chunk:(half + 1) * chunk] = partial[at:at + chunk]
             bsend[s, to, own:own + TAIL] = stats
-        for d in range(1, nx):
+        for d in far_x:
             to = lax.rem(x + d, nx)
             put(bsend.at[s, to], bbuf.at[s, x], b_sem.at[s, x], "section", to)
         bbuf[s, x] = bsend[s, x]
@@ -372,7 +375,7 @@
         ).start()
 
     back = sorted(
-        (turn + LAG * (sections - 1 - s), s, turn)
+        (turn + SCATTER_START[s], s, turn)
         for s in range(sections) for turn in range(stages(SCATTER_REACH[s]) + 1)
     )
 
@@ -391,10 +394,10 @@
         second_part = jnp.sum(exact * projb[s], axis=0, keepdims=True)
         dbuf[s, x, 0:own] = dproj
         dbuf[s, x, own:own + TAIL] = stat_rows(first_part, second_part)
-        for d in range(1, nx):
+        for d in far_x:
             put(dbuf.at[s, x], dbuf.at[s, x], d_sem.at[s, x], "section", lax.rem(x + d, nx))
         if turn > 0:
-            scatter_until(LAG * turn - 1)
+            scatter_until(2 * turn - 1)
         mean, inverse = meanb[s], invb[s]
         normed = (
             (abuf[s].reshape(deep, LANES).astype(F32) - mean) * inverse * gainb[s]
@@ -417,7 +420,7 @@
         for to in range(nt):
             qsend[s, to, 0:own] = product[to * own:(to + 1) * own]
             qsend[s, to, own:own + TAIL] = stats
-        for d in range(1, nt):
+        for d in far_t:
             to = lax.rem(t + d, nt)
             put(qsend.at[s, to], qbuf.at[s, t], q_sem.at[s, t], "tensor", to)
         qbuf[s, t] = qsend[s, t]
@@ -425,7 +428,7 @@
             normed, whole, (((1,), (1,)), ((), ())), preferred_element_type=F32
         )
         dwbuf[s] = term.astype(BF16).reshape(nz, chunk, width)
-        scatter_until(LAG * turn)
+        scatter_until(2 * turn)
         for d in range(1, nt):
             at = lax.rem(t + d, nt)
             got(qbuf.at[s, at], q_sem.at[s, at])
@@ -452,7 +455,7 @@
     for d in range(1, zb):
         to = group * zb + lax.rem(member + d, zb)
         put(v1.at[member], v1.at[member], v1_sem.at[member], "dp", to)
-    scatter_until(LAG * (sections - 1) + 1)
+    scatter_until(SCATTER_START[0] + 1)
     for d in range(1, zb):
         at = lax.rem(member + d, zb)
         got(v1.at[at], v1_sem.at[at])
@@ -460,7 +463,7 @@
     for d in range(1, za):
         to = lax.rem(group + d, za) * zb + member
         put(v2.at[group], v2.at[group], v2_sem.at[group], "dp", to)
-    scatter_until(LAG * (sections - 1) + 2)
+    scatter_until(SCATTER_START[0] + stages(SCATTER_REACH[0]) - 1)
     for d in range(1, za):
         at = lax.rem(group + d, za)
         got(v2.at[at], v2_sem.at[at])
@@ -468,9 +471,11 @@
     for at in range(1, za):
         full = full + v2[at]
     v3[x] = full
-    for d in range(1, nx):
+    for d in far_x:
         put(v3.at[x], v3.at[x], v3_sem.at[x], "section", lax.rem(x + d, nx))
-    scatter_until(LAG * sections + ups)
+    while back:
+        _, s, turn = back.pop(0)
+        scatter_event(s, turn)
     for d in range(1, nx):
         at = lax.rem(x + d, nx)
         got(v3.at[at], v3_sem.at[at])
@@ -482,13 +487,12 @@
             gain_row = jnp.where(x == s, tile[2 * s + 1:2 * s + 2], gain_row)
         for half in range(HALVES):
             to = half * (width // HALVES) + at * chunk
-            gate_out[0:1, to:to + chunk] = gate_row[:, half * chunk:(half + 1) * chunk]
-            gain_out[0:1, to:to + chunk] = gain_row[:, half * chunk:(half + 1) * chunk]
+            row_part[0:1, to:to + chunk] = gate_row[:, half * chunk:(half + 1) * chunk]
+            row_part[1:2, to:to + chunk] = gain_row[:, half * chunk:(half + 1) * chunk]
     for d in range(1, nx):
         at = lax.rem(x + d, nx)
         got(gw_in.at[at], gw_sem.at[at])
-    for at in range(nx):
-        gw_out[0, at * chunk:(at + 1) * chunk] = gw_in[at].astype(F32)
+    gw_part[...] = gw_in[...]
 
     for copy in sends:
         copy.wait_send()
@@ -499,6 +503,14 @@
                 src_ref=gw_send.at[s], dst_ref=gw_in.at[x], send_sem=local_sem.at[1 + s],
                 recv_sem=gw_sem.at[x], device_id={"section": s}, device_id_type=MESH,
             ).wait_send()
+
+
+def results(parts, rows, weight_out, gain_out, gate_out):
+    chunk = parts.shape[1]
+    for at in range(parts.shape[0]):
+        weight_out[0, at * chunk:(at + 1) * chunk] = parts[at].astype(F32)
+    gate_out[...] = rows[0:1]
+    gain_out[...] = rows[1:2]
 
 
 def local(inputs, velocity, weights, gains, gates, lengths, steps):
@@ -517,15 +529,14 @@
     dma = pltpu.SemaphoreType.DMA
     vmem = pl.BlockSpec(memory_space=pltpu.VMEM)
     anywhere = pl.BlockSpec(memory_space=pltpu.HBM)
-    return pl.pallas_call(
+    parts, rows = pl.pallas_call(
         functools.partial(kernel, nx, nt, nz),
         out_shape=(
-            jax.ShapeDtypeStruct((1, nx * chunk, width), F32),
-            jax.ShapeDtypeStruct((1, width), F32),
-            jax.ShapeDtypeStruct((1, width), F32),
+            jax.ShapeDtypeStruct((nx, chunk, width), BF16),
+            jax.ShapeDtypeStruct((2, width), F32),
         ),
         in_specs=[anywhere] * 7,
-        out_specs=(vmem, vmem, vmem),
+        out_specs=(vmem, vmem),
         scratch_shapes=[
             pltpu.VMEM(inputs.shape, BF16),
             pltpu.VMEM(velocity.shape, BF16),
@@ -585,6 +596,17 @@
         ),
         name="sections",
     )(weights, inputs, velocity, gains, gates, lengths, steps)
+    return pl.pallas_call(
+        results,
+        out_shape=(
+            jax.ShapeDtypeStruct((1, nx * chunk, width), F32),
+            jax.ShapeDtypeStruct((1, width), F32),
+            jax.ShapeDtypeStruct((1, width), F32),
+        ),
+        in_specs=[vmem, vmem],
+        out_specs=(vmem, vmem, vmem),
+        name="results",
+    )(parts, rows)
 
 
 def solution(mesh):

time: 141 us -> 133 us (0.943)
  the two profiles are of different devices: /device:TPU:16 before, /device:TPU:56 now
where the time goes in v4:
time: 133 us
  Pallas kernels  132 us (99%)
    pallas_call x1, Pallas kernels, local(): pl.pallas_call(functools.partial(kernel, nx, nt, nz), out_shape=(jax.Shap...  131 us

profile of v4, /device:TPU:56, one launch (start us, length us, event | category | flops | bytes accessed | tf_op | source)
XLA Modules:
  0.0 133.0 jit_solution(14730780092594614372)
XLA Ops:
  0.6 130.7 %sections.1 = (bf16[4,48,384]{2,1,0:T(8,128)(2,1)}, f32[2,384]{1,0:T(2,128)}) custom-call(bf16[1,192,384]{2,1,0:T(8,128)(2,1)} %w_in.1, bf16[4,40,384]{2,1,0:T(8,128)(2,1)} %inputs_in.1, bf16[4,40,384]{2,1,0:T(8,128)(2,1)} %velocity_in.1, f32[1,3072]{1,0:T(1,128)} %gains_in.1, f32[1,384]{1,0:T(1,128)} %gates_in.1, s32[1,4]{1,0:T(1,128)} %lengths_in.1, ...), custom_call_target="tpu_custom_call" | custom-call | tf_op jit(solution)/shard_map/sections/pallas_call | solution.py:532
  131.3 1.7 %results.1 = (f32[1,192,384]{2,1,0:T(8,128)}, f32[1,384]{1,0:T(1,128)}, f32[1,384]{1,0:T(1,128)}) custom-call(bf16[4,48,384]{2,1,0:T(8,128)(2,1)} %get-tuple-element.5.parts, f32[2,384]{1,0:T(2,128)} %get-tuple-element.6.rows), custom_call_target="tpu_custom_call" | custom-call | tf_op jit(solution)/shard_map/results/pallas_call | solution.py:599

commit v5 on v4

--- a/solution.py
+++ b/solution.py
@@ -19,8 +19,8 @@
 SMALL_ROWS = 24
 TAIL = 16
 PARTS_AT = 124
-GATHER_REACH = (2, 2, 1, 1)
-GATHER_START = (0, 2, 0, 2)
+GATHER_RELAYS = ((0, 2, 4, 6), (0, 1, 2, 3, 4, 6), (0, 1, 2, 3, 4, 5, 6, 7), (0, 1, 2, 3, 4, 5, 6, 7))
+GATHER_START = (0, 0, 1, 3)
 SCATTER_REACH = (2, 2, 2, 2)
 SCATTER_START = (6, 4, 2, 0)
 
@@ -82,7 +82,7 @@
     for d in range(1, nx):
         greet("section", lax.rem(x + d, nx))
         greeted += 1
-    far = max(GATHER_REACH + SCATTER_REACH)
+    far = max(SCATTER_REACH)
     for d in range(1, far + 1):
         greet("dp", lax.rem(z + d, nz))
         greet("dp", lax.rem(z + nz - d, nz))
@@ -153,27 +153,31 @@
     def stages(reach):
         return -(-ups // reach)
 
+    def lanes_of(s, up, down):
+        first, second = (ups, downs) if s % 2 == 0 else (downs, ups)
+        return (1, first, up), (-1, second, down)
+
     def gather_event(s, j):
-        reach = GATHER_REACH[s]
+        relays = [r for r in GATHER_RELAYS[s] if r < ups]
         if j == 0:
             wait_piece(s)
-        for way, total, sem in ((1, ups, up_sem), (-1, downs, down_sem)):
-            gone = j * reach
-            if j == stages(reach):
+        for way, total, sem in lanes_of(s, up_sem, down_sem):
+            if j == len(relays):
                 for q in range(1, total + 1):
-                    if q % reach or q >= total:
+                    if q not in relays:
                         got(wbuf.at[s, lax.rem(z - way * q + nz, nz)], sem.at[s, q - 1])
                 continue
-            if gone >= total:
-                continue
+            gone = relays[j]
+            last = min(total, (relays + [ups])[j + 1])
             piece = wbuf.at[s, lax.rem(z - way * gone + nz, nz)]
-            if j > 0:
+            if 0 < gone <= total:
                 got(piece, sem.at[s, gone - 1])
-            for d in range(min(reach, total - gone), 0, -1):
+            for d in range(last - gone, 0, -1):
                 put(piece, piece, sem.at[s, gone + d - 1], "dp", lax.rem(z + way * d + nz, nz))
 
     events = sorted(
-        (j + GATHER_START[s], s, j) for s in range(sections) for j in range(stages(GATHER_REACH[s]) + 1)
+        (j + GATHER_START[s], s, j) for s in range(sections)
+        for j in range(sum(r < ups for r in GATHER_RELAYS[s]) + 1)
     )
 
     def gather_until(key):
@@ -252,7 +256,7 @@
     factor = jnp.where(lane < LIVE_PER_CLIP, factor, 0.0)
 
     def key_after(s):
-        return stages(GATHER_REACH[0]) + 2 * s + 1
+        return len(GATHER_RELAYS[0]) + 2 * s + 1
 
     coeff = math.sqrt(2.0 / math.pi)
     state = None
@@ -332,17 +336,14 @@
 
     def scatter_event(s, turn):
         reach = SCATTER_REACH[s]
-        relay = stages(reach) - turn
+        count = stages(reach)
+        relay = count - turn
         mine = dwbuf[s, z].astype(F32) if relay == 0 else None
-        for way, total, slots, sem in ((1, ups, rs_up, rsu_sem), (-1, downs, rs_down, rsd_sem)):
-            if turn == 0:
-                for q in range(total, 0, -1):
-                    if q % reach and q > 0 or q == total:
-                        d = q - reach * ((q - 1) // reach)
-                        to = lax.rem(z + way * d + nz, nz)
-                        term = dwbuf.at[s, lax.rem(z + way * q + nz, nz)]
-                        put(term, slots.at[s, q - 1], sem.at[s, q - 1], "dp", to)
-                continue
+        ways = [
+            (way, total, slots, sem)
+            for way, total, (slots, sem) in lanes_of(s, (rs_up, rsu_sem), (rs_down, rsd_sem))
+        ]
+        for way, total, slots, sem in ways if turn > 0 else ():
             gone = relay * reach
             if gone >= total:
                 continue
@@ -357,6 +358,14 @@
                 slots[s, gone] = mine.astype(BF16)
                 to = lax.rem(z + way * reach + nz, nz)
                 put(slots.at[s, gone], slots.at[s, gone - 1], sem.at[s, gone - 1], "dp", to)
+        groups = (count, count - 1) if turn == 0 else (relay - 1,)
+        for level in groups:
+            for way, total, slots, sem in ways:
+                for q in range(min(level * reach, total), (level - 1) * reach, -1):
+                    if level >= 1 and (q % reach or q == total):
+                        to = lax.rem(z + way * (q - (level - 1) * reach) + nz, nz)
+                        term = dwbuf.at[s, lax.rem(z + way * q + nz, nz)]
+                        put(term, slots.at[s, q - 1], sem.at[s, q - 1], "dp", to)
         if relay == 0:
             gw_send[s] = mine.astype(BF16)
 
@@ -415,6 +424,16 @@
             one, two = joined(dbuf[s, at, own:own + TAIL])
             first_sum += one
             second_sum += two
+        def weight_term():
+            term = lax.dot_general(
+                normed, whole, (((1,), (1,)), ((), ())), preferred_element_type=F32
+            )
+            dwbuf[s] = term.astype(BF16).reshape(nz, chunk, width)
+
+        if s == 0:
+            weight_term()
+            assert back.pop(0)[1:] == (0, 0)
+            scatter_event(0, 0)
         product = jnp.dot(wbuf[s].reshape(deep, width), whole, preferred_element_type=F32).astype(BF16)
         stats = stat_rows(first_sum, second_sum)
         for to in range(nt):
@@ -424,10 +443,8 @@
             to = lax.rem(t + d, nt)
             put(qsend.at[s, to], qbuf.at[s, t], q_sem.at[s, t], "tensor", to)
         qbuf[s, t] = qsend[s, t]
-        term = lax.dot_general(
-            normed, whole, (((1,), (1,)), ((), ())), preferred_element_type=F32
-        )
-        dwbuf[s] = term.astype(BF16).reshape(nz, chunk, width)
+        if s > 0:
+            weight_term()
         scatter_until(2 * turn)
         for d in range(1, nt):
             at = lax.rem(t + d, nt)
@@ -566,7 +583,7 @@
             pltpu.VMEM((sections, nt, block, LANES), BF16),
             pltpu.VMEM((sections, nz, chunk, width), BF16),
             pltpu.VMEM((sections, ups, chunk, width), BF16),
-            pltpu.VMEM((sections, max(downs, 1), chunk, width), BF16),
+            pltpu.VMEM((sections, ups, chunk, width), BF16),
             pltpu.VMEM((sections, chunk, width), BF16),
             pltpu.VMEM((nx, chunk, width), BF16),
             pltpu.VMEM((LANES, LANES), F32),
@@ -579,13 +596,13 @@
             dma((nx,)),
             dma((nx,)),
             dma((sections, ups)),
-            dma((sections, max(downs, 1))),
+            dma((sections, ups)),
             dma((sections, nt)),
             dma((sections, nx)),
             dma((sections, nx)),
             dma((sections, nt)),
             dma((sections, ups)),
-            dma((sections, max(downs, 1))),
+            dma((sections, ups)),
             dma((nx,)),
             dma((4,)),
             dma((max(nz // 4, 1),)),

time: 133 us -> 129 us (0.970)
  the two profiles are of different devices: /device:TPU:56 before, /device:TPU:16 now
where the time goes in v5:
time: 129 us
  Pallas kernels  128 us (99%)
    pallas_call x1, Pallas kernels, local(): pl.pallas_call(functools.partial(kernel, nx, nt, nz), out_shape=(jax.Shap...  127 us

profile of v5, /device:TPU:16, one launch (start us, length us, event | category | flops | bytes accessed | tf_op | source)
XLA Modules:
  0.0 128.8 jit_solution(7754666813426140527)
XLA Ops:
  0.6 126.5 %sections.1 = (bf16[4,48,384]{2,1,0:T(8,128)(2,1)}, f32[2,384]{1,0:T(2,128)}) custom-call(bf16[1,192,384]{2,1,0:T(8,128)(2,1)} %w_in.1, bf16[4,40,384]{2,1,0:T(8,128)(2,1)} %inputs_in.1, bf16[4,40,384]{2,1,0:T(8,128)(2,1)} %velocity_in.1, f32[1,3072]{1,0:T(1,128)} %gains_in.1, f32[1,384]{1,0:T(1,128)} %gates_in.1, s32[1,4]{1,0:T(1,128)} %lengths_in.1, ...), custom_call_target="tpu_custom_call" | custom-call | tf_op jit(solution)/shard_map/sections/pallas_call | solution.py:549
  127.2 1.7 %results.1 = (f32[1,192,384]{2,1,0:T(8,128)}, f32[1,384]{1,0:T(1,128)}, f32[1,384]{1,0:T(1,128)}) custom-call(bf16[4,48,384]{2,1,0:T(8,128)(2,1)} %get-tuple-element.5.parts, f32[2,384]{1,0:T(2,128)} %get-tuple-element.6.rows), custom_call_target="tpu_custom_call" | custom-call | tf_op jit(solution)/shard_map/results/pallas_call | solution.py:616

commit v6 on v5

--- a/solution.py
+++ b/solution.py
@@ -19,8 +19,8 @@
 SMALL_ROWS = 24
 TAIL = 16
 PARTS_AT = 124
-GATHER_RELAYS = ((0, 2, 4, 6), (0, 1, 2, 3, 4, 6), (0, 1, 2, 3, 4, 5, 6, 7), (0, 1, 2, 3, 4, 5, 6, 7))
-GATHER_START = (0, 0, 1, 3)
+GATHER_RELAYS = ((0, 3, 6), (0, 1, 2, 3, 4, 6), (0, 1, 2, 3, 4, 5, 6, 7), (0, 1, 2, 3, 4, 5, 6, 7))
+GATHER_START = (0, 0, 0, 2)
 SCATTER_REACH = (2, 2, 2, 2)
 SCATTER_START = (6, 4, 2, 0)
 
@@ -82,7 +82,7 @@
     for d in range(1, nx):
         greet("section", lax.rem(x + d, nx))
         greeted += 1
-    far = max(SCATTER_REACH)
+    far = 3
     for d in range(1, far + 1):
         greet("dp", lax.rem(z + d, nz))
         greet("dp", lax.rem(z + nz - d, nz))
@@ -102,6 +102,14 @@
         )
         copy.start()
         sends.append(copy)
+
+    finished = []
+
+    def finish_sends(count):
+        while len(finished) < count:
+            copy = sends[len(finished)]
+            copy.wait_send()
+            finished.append(copy)
 
     def got(dst, recv):
         pltpu.make_async_remote_copy(
@@ -397,6 +405,7 @@
         vacc[0:own] = jnp.where(
             lane == 2 * s, jnp.sum(upstream * gelub[s], axis=1, keepdims=True), vacc[0:own]
         )
+        older = len(sends)
         dproj = (upstream * slopeb[s]).astype(BF16)
         exact = dproj.astype(F32)
         first_part = jnp.sum(exact * ub[s], axis=0, keepdims=True)
@@ -446,6 +455,7 @@
         if s > 0:
             weight_term()
         scatter_until(2 * turn)
+        finish_sends(older)
         for d in range(1, nt):
             at = lax.rem(t + d, nt)
             got(qbuf.at[s, at], q_sem.at[s, at])
@@ -473,6 +483,7 @@
         to = group * zb + lax.rem(member + d, zb)
         put(v1.at[member], v1.at[member], v1_sem.at[member], "dp", to)
     scatter_until(SCATTER_START[0] + 1)
+    finish_sends(len(sends) - 20)
     for d in range(1, zb):
         at = lax.rem(member + d, zb)
         got(v1.at[at], v1_sem.at[at])
@@ -488,6 +499,7 @@
     for at in range(1, za):
         full = full + v2[at]
     v3[x] = full
+    finish_sends(len(sends) - 6)
     for d in far_x:
         put(v3.at[x], v3.at[x], v3_sem.at[x], "section", lax.rem(x + d, nx))
     while back:
@@ -511,8 +523,7 @@
         got(gw_in.at[at], gw_sem.at[at])
     gw_part[...] = gw_in[...]
 
-    for copy in sends:
-        copy.wait_send()
+    finish_sends(len(sends))
     for s in range(sections):
         @pl.when(x != s)
         def _():

time: 129 us -> 129 us (level)
  the two profiles are of different devices: /device:TPU:16 before, /device:TPU:64 now
where the time goes in v6:
time: 129 us
  Pallas kernels  128 us (99%)
    pallas_call x1, Pallas kernels, local(): pl.pallas_call(functools.partial(kernel, nx, nt, nz), out_shape=(jax.Shap...  126 us

profile of v6, /device:TPU:64, one launch (start us, length us, event | category | flops | bytes accessed | tf_op | source)
XLA Modules:
  0.0 128.7 jit_solution(5961893896827674495)
XLA Ops:
  0.6 126.4 %sections.1 = (bf16[4,48,384]{2,1,0:T(8,128)(2,1)}, f32[2,384]{1,0:T(2,128)}) custom-call(bf16[1,192,384]{2,1,0:T(8,128)(2,1)} %w_in.1, bf16[4,40,384]{2,1,0:T(8,128)(2,1)} %inputs_in.1, bf16[4,40,384]{2,1,0:T(8,128)(2,1)} %velocity_in.1, f32[1,3072]{1,0:T(1,128)} %gains_in.1, f32[1,384]{1,0:T(1,128)} %gates_in.1, s32[1,4]{1,0:T(1,128)} %lengths_in.1, ...), custom_call_target="tpu_custom_call" | custom-call | tf_op jit(solution)/shard_map/sections/pallas_call | solution.py:560
  127.1 1.7 %results.1 = (f32[1,192,384]{2,1,0:T(8,128)}, f32[1,384]{1,0:T(1,128)}, f32[1,384]{1,0:T(1,128)}) custom-call(bf16[4,48,384]{2,1,0:T(8,128)(2,1)} %get-tuple-element.5.parts, f32[2,384]{1,0:T(2,128)} %get-tuple-element.6.rows), custom_call_target="tpu_custom_call" | custom-call | tf_op jit(solution)/shard_map/results/pallas_call | solution.py:627

commit v7 on v6

--- a/solution.py
+++ b/solution.py
@@ -269,9 +269,6 @@
     coeff = math.sqrt(2.0 / math.pi)
     state = None
     for s in range(sections):
-        if s > 0:
-            abuf[s, t] = state
-            a_sends(s)
         gather_all_of(s)
         weight = wbuf[s].reshape(deep, width)
         wt[...] = jnp.transpose(weight)
@@ -325,17 +322,20 @@
         v = total * inverse
         tanh = jnp.tanh(coeff * (v + 0.044715 * v * v * v))
         gelu = 0.5 * v * (1.0 + tanh)
+        gate = gateb[s]
+        state = (abuf[s, t].astype(F32) + gate * gelu).astype(BF16)
+        if s < sections - 1:
+            abuf[s + 1, t] = state
+            a_sends(s + 1)
         slope = 0.5 * (1.0 + tanh) + 0.5 * v * (1.0 - tanh * tanh) * coeff * (
             1.0 + 3.0 * 0.044715 * v * v
         )
-        gate = gateb[s]
         projb[s] = v
         gelub[s] = gelu
         slopeb[s] = gate * slope
         meanb[s] = mean
         invb[s] = inverse
         ub[s] = jnp.broadcast_to(sum(sums[1:], sums[0]), (own, LANES))
-        state = (abuf[s, t].astype(F32) + gate * gelu).astype(BF16)
 
 
     target = own_part(1).astype(F32)
@@ -401,10 +401,12 @@
             _, s, turn = back.pop(0)
             scatter_event(s, turn)
 
+    def add_gain(s, dnormed, xhat):
+        vacc[0:own] = jnp.where(
+            lane == 2 * s + 1, jnp.sum(dnormed * xhat, axis=1, keepdims=True), vacc[0:own]
+        )
+
     for turn, s in enumerate(reversed(range(sections))):
-        vacc[0:own] = jnp.where(
-            lane == 2 * s, jnp.sum(upstream * gelub[s], axis=1, keepdims=True), vacc[0:own]
-        )
         older = len(sends)
         dproj = (upstream * slopeb[s]).astype(BF16)
         exact = dproj.astype(F32)
@@ -416,6 +418,11 @@
             put(dbuf.at[s, x], dbuf.at[s, x], d_sem.at[s, x], "section", lax.rem(x + d, nx))
         if turn > 0:
             scatter_until(2 * turn - 1)
+        vacc[0:own] = jnp.where(
+            lane == 2 * s, jnp.sum(upstream * gelub[s], axis=1, keepdims=True), vacc[0:own]
+        )
+        if turn > 0:
+            add_gain(s + 1, dnormed, xhat)
         mean, inverse = meanb[s], invb[s]
         normed = (
             (abuf[s].reshape(deep, LANES).astype(F32) - mean) * inverse * gainb[s]
@@ -468,9 +475,6 @@
             first_moment += one
             second_moment += two
         xhat = (abuf[s, t].astype(F32) - mean) * inverse
-        vacc[0:own] = jnp.where(
-            lane == 2 * s + 1, jnp.sum(dnormed * xhat, axis=1, keepdims=True), vacc[0:own]
-        )
         if s > 0:
             gain = gainb[s, pl.ds(pl.multiple_of(t * own, 8), own)]
             change = dnormed * gain - first_moment * (1.0 / model) - xhat * (
@@ -478,6 +482,7 @@
             )
             upstream = (upstream + inverse * change).astype(BF16).astype(F32)
 
+    add_gain(0, dnormed, xhat)
     v1[member] = jnp.transpose(vacc[...])[0:8]
     for d in range(1, zb):
         to = group * zb + lax.rem(member + d, zb)

time: 129 us -> 129 us (level)
  no operation moved by 1% of the time
where the time goes in v7:
time: 129 us; the launch traced here: 128 us
  Pallas kernels  128 us (99%)
    pallas_call x1, Pallas kernels, local(): pl.pallas_call(functools.partial(kernel, nx, nt, nz), out_shape=(jax.Shap...  126 us

profile of v7, /device:TPU:64, one launch (start us, length us, event | category | flops | bytes accessed | tf_op | source)
XLA Modules:
  0.0 128.4 jit_solution(3709570486767418944)
XLA Ops:
  0.6 126.2 %sections.1 = (bf16[4,48,384]{2,1,0:T(8,128)(2,1)}, f32[2,384]{1,0:T(2,128)}) custom-call(bf16[1,192,384]{2,1,0:T(8,128)(2,1)} %w_in.1, bf16[4,40,384]{2,1,0:T(8,128)(2,1)} %inputs_in.1, bf16[4,40,384]{2,1,0:T(8,128)(2,1)} %velocity_in.1, f32[1,3072]{1,0:T(1,128)} %gains_in.1, f32[1,384]{1,0:T(1,128)} %gates_in.1, s32[1,4]{1,0:T(1,128)} %lengths_in.1, ...), custom_call_target="tpu_custom_call" | custom-call | tf_op jit(solution)/shard_map/sections/pallas_call | solution.py:565
  126.8 1.7 %results.1 = (f32[1,192,384]{2,1,0:T(8,128)}, f32[1,384]{1,0:T(1,128)}, f32[1,384]{1,0:T(1,128)}) custom-call(bf16[4,48,384]{2,1,0:T(8,128)(2,1)} %get-tuple-element.5.parts, f32[2,384]{1,0:T(2,128)} %get-tuple-element.6.rows), custom_call_target="tpu_custom_call" | custom-call | tf_op jit(solution)/shard_map/results/pallas_call | solution.py:632
